TPU v7x, 32 devices: a whole 2x2x4 slice. The times are simulated.
32 devices in a mesh: rows: 8 (over y, x, core), heads: 4 (over z).
Axes of the slice: x: 2, y: 2, z: 4, core: 2. Of those that a mesh axis runs over, the one named last changes fastest.
Arguments:
- images: bfloat16 [16, 64, 64, 512], P('heads', 'rows'), may hold values from -6 to 6
- image_sides: int32 [16], replicated, may hold values from 32 to 64, as said below
- labels: int32 [16], replicated, may hold values from 0 to 999
- timesteps: int32 [16], replicated, may hold values from 0 to 999
- cotangent: bfloat16 [16, 64, 64, 512], P('heads', 'rows'), may hold values from -6 to 6
- first_gain: bfloat16 [512], replicated, may hold values from 0.25 to 1.75
- first_bias: bfloat16 [512], replicated, may hold values from -3 to 3
- conv_one: bfloat16 [4608, 512], replicated, may hold values from -0.09375 to 0.09375
- time_proj: bfloat16 [1024, 512], replicated, may hold values from -0.5 to 0.5
- time_bias: bfloat16 [512], replicated, may hold values from -3 to 3
- second_gain: bfloat16 [512], replicated, may hold values from 0.25 to 1.75
- second_bias: bfloat16 [512], replicated, may hold values from -3 to 3
- conv_two: bfloat16 [4608, 512], replicated, may hold values from -0.09375 to 0.09375
- conv_bias: bfloat16 [512], replicated, may hold values from -3 to 3
- third_gain: bfloat16 [512], replicated, may hold values from 0.25 to 1.75
- third_bias: bfloat16 [512], replicated, may hold values from -3 to 3
- proj_in: bfloat16 [512, 512], replicated, may hold values from -0.25 to 0.25
- proj_in_bias: bfloat16 [512], replicated, may hold values from -3 to 3
- attn_gain: bfloat16 [512], replicated, may hold values from 0.25 to 1.75
- attn_bias: bfloat16 [512], replicated, may hold values from -3 to 3
- qkv_proj: bfloat16 [512, 1536], replicated, may hold values from -0.25 to 0.25
- attn_out: bfloat16 [512, 512], replicated, may hold values from -16 to 16
- attn_out_bias: bfloat16 [512], replicated, may hold values from -6 to 6
- class_table: bfloat16 [1000, 512], replicated, may hold values from -6 to 6
- cross_value: bfloat16 [512, 512], replicated, may hold values from -0.25 to 0.25
- cross_out: bfloat16 [512, 512], replicated, may hold values from -0.25 to 0.25
- feed_gain: bfloat16 [512], replicated, may hold values from 0.25 to 1.75
- feed_bias: bfloat16 [512], replicated, may hold values from -3 to 3
- geglu_proj: bfloat16 [512, 4096], replicated, may hold values from -0.25 to 0.25
- geglu_bias: bfloat16 [4096], replicated, may hold values from -3 to 3
- feed_out: bfloat16 [2048, 512], replicated, may hold values from -0.1875 to 0.1875
- feed_out_bias: bfloat16 [512], replicated, may hold values from -7 to 7
- proj_out: bfloat16 [512, 512], replicated, may hold values from -0.25 to 0.25
- proj_out_bias: bfloat16 [512], replicated, may hold values from -6 to 6
Outputs:
- output: bfloat16 [16, 64, 64, 512], P('heads', 'rows')
- grad_images: float32 [16, 64, 64, 512], P('heads', 'rows')
- grad_first_gain: float32 [512], P('rows')
- grad_first_bias: float32 [512], P('rows')
- grad_conv_one: float32 [4608, 512], P('rows')
- grad_time_proj: float32 [1024, 512], P('rows')
- grad_time_bias: float32 [512], P('rows')
- grad_second_gain: float32 [512], P('rows')
- grad_second_bias: float32 [512], P('rows')
- grad_conv_two: float32 [4608, 512], P('rows')
- grad_conv_bias: float32 [512], P('rows')
- grad_third_gain: float32 [512], P('rows')
- grad_third_bias: float32 [512], P('rows')
- grad_proj_in: float32 [512, 512], P('rows')
- grad_proj_in_bias: float32 [512], P('rows')
- grad_attn_gain: float32 [512], P('rows')
- grad_attn_bias: float32 [512], P('rows')
- grad_qkv_proj: float32 [512, 1536], P('rows')
- grad_attn_out: float32 [512, 512], P('rows')
- grad_attn_out_bias: float32 [512], P('rows')
- grad_class_table: float32 [1000, 512], P(None, 'rows')
- grad_cross_value: float32 [512, 512], P('rows')
- grad_cross_out: float32 [512, 512], P('rows')
- grad_feed_gain: float32 [512], P('rows')
- grad_feed_bias: float32 [512], P('rows')
- grad_geglu_proj: float32 [512, 4096], P('rows')
- grad_geglu_bias: float32 [4096], P('rows')
- grad_feed_out: float32 [2048, 512], P('rows')
- grad_feed_out_bias: float32 [512], P('rows')
- grad_proj_out: float32 [512, 512], P('rows')
- grad_proj_out_bias: float32 [512], P('rows')
Inputs may be any that keep to these rules, and one draw needn't show every extreme that they name: `image_sides`: each side is 64, 48 or 32; each block of 4 consecutive images holds at least one of side 64.
All inputs are finite; a program needn't handle non-finite values.
Results may differ from a plain program's by a relative error of at most 0.018.
Values may be sent and summed in bfloat16 or wider, within the bound.
A program may use at most 640 MiB of HBM per device.

v0:
```python
from functools import partial
import math

import jax
import jax.numpy as jnp
from jax import lax
from jax.experimental import pallas as pl
from jax.experimental.pallas import tpu as pltpu
from jax.sharding import PartitionSpec as P

HEADS = 8
GROUPS = 32
GN_EPS = 1e-06
LN_EPS = 1e-05
HIGH = lax.Precision.HIGHEST
LOG2E = math.log2(math.e)
BF = jnp.bfloat16
F32 = jnp.float32
KEPT = 256
APART = 80

def dot_nt(lhs, rhs):
    return lax.dot_general(lhs, rhs, (((1,), (1,)), ((), ())), preferred_element_type=F32)


def dot_nn(lhs, rhs):
    return lax.dot_general(lhs, rhs, (((1,), (0,)), ((), ())), preferred_element_type=F32)


def lane_ids(rows):
    return lax.broadcasted_iota(jnp.int32, (rows, 128), 1)


def swap_halves(field):
    return pltpu.roll(field, 64, 1)


def pieces_of(column):
    top = column.astype(BF).astype(F32)
    rest = column - top
    mid = rest.astype(BF).astype(F32)
    return (top, mid, rest - mid)


def extras(column, lanes, first):
    top, mid, low = pieces_of(column)
    return jnp.where(
        lanes == first, top, jnp.where(lanes == first + 1, mid, jnp.where(lanes == first + 2, low, 0.0))
    )


def block_of(count, pref):
    for size in pref:
        if count % size == 0:
            return size
    return count


def crop(field, width, side):
    rows = field.shape[0] // width
    if side == width:
        return field
    return field.reshape(rows, width, 128)[:, :side].reshape(rows * side, 128)


def uncrop(field, width, side):
    if side == width:
        return field
    rows = field.shape[0] // side
    spread = field.reshape(rows, side, 128)
    return jnp.concatenate(
        [spread, jnp.zeros((rows, width - side, 128), field.dtype)], axis=1
    ).reshape(rows * width, 128)


def unpack_pairs(pairs):
    return jnp.concatenate([pairs, swap_halves(pairs)], axis=0)


def pack_pairs(field, lanes):
    half = field.shape[0] // 2
    return jnp.where(lanes[:half] < 64, field[:half], swap_halves(field[half:]))


def attend_kernel(width, scale, side_ref, qkv_ref, out_ref, norm_ref, kept_ref, q_s, k_s, v_s, vt_s, top_s, stage_s, sems):
    bands, packed, _ = qkv_ref.shape
    band_tokens = packed * 2 // 3
    band_rows = band_tokens // width
    side_now = side_ref[0]

    def variant(side):
        tokens = side * side
        used = side // band_rows
        own = band_rows * side
        lanes = lane_ids(own)
        low = lanes < 64
        row_ids = lax.broadcasted_iota(jnp.int32, (128, 128), 0)
        col_ids = lax.broadcasted_iota(jnp.int32, (128, 128), 1)
        picks = jnp.where((row_ids < 64) == (col_ids < 64), 1.0, 0.0).astype(BF)

        def gather_band(band, norms):
            pairs = crop(qkv_ref[band, band_tokens:, :].astype(F32), width, side)
            keys = crop(qkv_ref[band, :band_tokens, :].astype(F32), width, side)
            queries = unpack_pairs(pairs) * (scale * LOG2E)
            head = queries.astype(BF).astype(F32)
            turned = swap_halves(keys)
            rows = pl.ds(pl.multiple_of(band * own, 16), own)
            q_s[rows, :] = jnp.where(low, head, swap_halves(queries - head)).astype(BF)
            k_s[rows, :] = jnp.where(low, keys, turned).astype(BF)
            v_s[rows, :] = jnp.where(low, turned, jnp.where(lanes == 64, 1.0, 0.0)).astype(BF)
            joint = jnp.where(low, queries, turned)
            sums = dot_nn((joint * joint).astype(BF), picks)
            return jnp.maximum(norms, jnp.max(sums, axis=0, keepdims=True))

        norms = lax.fori_loop(0, used, gather_band, jnp.zeros((1, 128), F32))
        step = block_of(tokens, (512, 256))
        for first in range(0, tokens, step):
            vt_s[:, first : first + step] = v_s[first : first + step, :].T
        first_lanes = lane_ids(1) < 64
        query_top = jnp.max(jnp.where(first_lanes, norms, 0.0))
        key_top = jnp.max(jnp.where(first_lanes, 0.0, norms))
        safe = query_top * key_top * 1.05 <= 100.0 * 100.0
        bq = block_of(tokens, (1024, 768, 256))
        bk = block_of(tokens, (1024, 768, 256))

        @pl.when(safe)
        def _():
            top_s[...] = jnp.zeros_like(top_s)

        @pl.when(jnp.logical_not(safe))
        def _():
            def tops(qi, _):
                cols = pl.ds(pl.multiple_of(qi * bq, 256), bq)
                queries = q_s[cols, :]

                def more(ki, top):
                    scores = dot_nt(k_s[pl.ds(pl.multiple_of(ki * bk, 256), bk), :], queries)
                    return jnp.maximum(top, jnp.max(scores, axis=0, keepdims=True))

                top = lax.fori_loop(0, tokens // bk, more, jnp.full((1, bq), -jnp.inf, F32))
                top_s[:, cols] = jnp.broadcast_to(top, (8, bq))
                return 0

            lax.fori_loop(0, tokens // bq, tops, 0)

        parts = bq // KEPT
        steps = tokens // bq
        slots = min(steps, stage_s.shape[0] // tokens, 3)

        def stores(qi, first=0, rows=tokens):
            slot = lax.rem(qi, slots)
            return [
                pltpu.make_async_copy(
                    stage_s.at[pl.ds(pl.multiple_of(slot * tokens + first, 128), rows), pl.ds(part * KEPT, KEPT)],
                    kept_ref.at[pl.ds(pl.multiple_of((qi * parts + part) * (tokens + APART) + first, 16), rows)],
                    sems.at[slot, part],
                )
                for part in range(parts)
            ]

        def main(qi, _):
            cols = pl.ds(pl.multiple_of(qi * bq, 256), bq)
            queries = q_s[cols, :]
            top = top_s[0:1, cols]
            slot = lax.rem(qi, slots)

            @pl.when(qi >= slots)
            def _():
                for item in stores(qi - slots):
                    item.wait()

            total = jnp.zeros((80, bq), F32)
            for first in range(0, tokens, bk):
                scores = dot_nt(k_s[first : first + bk, :], queries)
                weights = jnp.exp2(scores - top).astype(BF)
                stage_s[pl.ds(pl.multiple_of(slot * tokens + first, 128), bk), :bq] = weights
                total = total + dot_nn(vt_s[0:80, first : first + bk], weights)
                for item in stores(qi, first, bk):
                    item.start()
            row_total = total[64:65]
            mixed = total[:64] / row_total
            extra = jnp.broadcast_to(1.0 / row_total, (64, bq))
            norm_ref[cols, :] = jnp.concatenate([mixed, extra], axis=0).T
            return 0

        lax.fori_loop(0, steps, main, 0)
        for qi in range(steps - slots, steps):
            for item in stores(qi):
                item.wait()

        def spread_band(band, _):
            rows = pl.ds(pl.multiple_of(band * own, 16), own)
            pairs = pack_pairs(norm_ref[rows, :], lanes)
            out_ref[band] = uncrop(pairs, width, side).astype(BF)
            return 0

        lax.fori_loop(0, used, spread_band, 0)
        if used < bands:
            out_ref[used:] = jnp.zeros((bands - used,) + out_ref.shape[1:], BF)

    for side in (width, width * 3 // 4, width // 2):
        pl.when(side_now == side)(partial(variant, side))


def attend(side, qkv, width, scale):
    bands, packed, _ = qkv.shape
    tokens = bands * packed * 2 // 3
    vm = pl.BlockSpec(memory_space=pltpu.VMEM)
    return pl.pallas_call(
        partial(attend_kernel, width, scale),
        out_shape=(
            jax.ShapeDtypeStruct((bands, packed // 3, 128), BF),
            jax.ShapeDtypeStruct((tokens, 128), F32),
            jax.ShapeDtypeStruct((tokens // KEPT * (tokens + APART), KEPT), BF),
        ),
        in_specs=[pl.BlockSpec(memory_space=pltpu.SMEM), vm],
        out_specs=(vm, vm, pl.BlockSpec(memory_space=pl.ANY)),
        scratch_shapes=[
            pltpu.VMEM((tokens, 128), BF),
            pltpu.VMEM((tokens, 128), BF),
            pltpu.VMEM((tokens, 128), BF),
            pltpu.VMEM((128, tokens), BF),
            pltpu.VMEM((8, tokens), F32),
            pltpu.VMEM((2 * tokens, 1024), BF),
            pltpu.SemaphoreType.DMA((3, 4)),
        ],
        compiler_params=pltpu.CompilerParams(vmem_limit_bytes=62 << 20),
        cost_estimate=pl.CostEstimate(
            flops=4 * 256 * tokens * tokens, bytes_accessed=8 << 20, transcendentals=tokens * tokens
        ),
        name="attend",
    )(side, qkv)


def attend_back_kernel(width, scale, side_ref, qkv_ref, grad_ref, norm_ref, kept_ref, out_ref,
                       k_s, g_s, gn_s, v_s, q_s, kt_s, dq_s, dkv_s, recip_s, stage_s, sems):
    bands, packed, _ = qkv_ref.shape
    band_tokens = packed * 2 // 3
    band_rows = band_tokens // width
    side_now = side_ref[0]

    def variant(side):
        tokens = side * side
        used = side // band_rows
        own = band_rows * side
        lanes = lane_ids(own)
        low = lanes < 64
        ones_high = jnp.where((lanes >= 64) & (lanes < 67), 1.0, 0.0)
        bq = block_of(tokens, (1024, 768, 256))
        bk = block_of(tokens, (512, 768, 256))
        parts = bq // KEPT
        steps = tokens // bq
        slots = min(steps, stage_s.shape[0] // tokens, 3)

        def loads(qi):
            slot = lax.rem(qi, slots)
            return [
                pltpu.make_async_copy(
                    kept_ref.at[pl.ds(pl.multiple_of((qi * parts + part) * (tokens + APART), 16), tokens)],
                    stage_s.at[pl.ds(pl.multiple_of(slot * tokens, 128), tokens), pl.ds(part * KEPT, KEPT)],
                    sems.at[slot, part],
                )
                for part in range(parts)
            ]

        ahead = steps if slots == steps else slots - 1
        for qi in range(ahead):
            for item in loads(qi):
                item.start()

        def gather_band(band, _):
            queries = unpack_pairs(crop(qkv_ref[band, band_tokens:, :].astype(F32), width, side))
            keys = crop(qkv_ref[band, :band_tokens, :].astype(F32), width, side)
            grads = unpack_pairs(crop(grad_ref[0, band].astype(F32), width, side))
            rows = pl.ds(pl.multiple_of(band * own, 16), own)
            mixed = norm_ref[rows, :]
            delta = jnp.sum(jnp.where(low, grads * mixed, 0.0), axis=1, keepdims=True)
            turned = swap_halves(keys)
            q_s[rows, :] = jnp.where(low, 0.0, swap_halves(queries)).astype(BF)
            gn_s[rows, :] = jnp.where(low, grads, 0.0).astype(BF)
            g_s[rows, :] = jnp.where(low, grads, extras(-delta, lanes, 64)).astype(BF)
            v_s[rows, :] = jnp.where(low, turned, ones_high).astype(BF)
            k_s[rows, :] = jnp.where(low, keys, 0.0).astype(BF)
            return 0

        lax.fori_loop(0, used, gather_band, 0)
        step = block_of(tokens, (512, 256))
        for first in range(0, tokens, step):
            kt_s[:, first : first + step] = k_s[first : first + step, :].T[:64]
            recip_s[:, first : first + step] = norm_ref[first : first + step, :].T[64:72]
        dkv_s[...] = jnp.zeros_like(dkv_s)

        def main(qi, _):
            cols = pl.ds(pl.multiple_of(qi * bq, 256), bq)
            slot = lax.rem(qi, slots)
            for item in loads(qi):
                item.wait()

            @pl.when(qi + ahead < steps)
            def _():
                for item in loads(qi + ahead):
                    item.start()

            grads = g_s[cols, :]
            plain = gn_s[cols, :]
            queries = q_s[cols, :]
            recip = recip_s[0:1, cols]
            total = jnp.zeros((64, bq), F32)
            for first in range(0, tokens, bk):
                lines = pl.ds(pl.multiple_of(slot * tokens + first, 128), bk)
                probs = stage_s[lines, :bq].astype(F32) * recip
                slopes = dot_nt(v_s[first : first + bk, :], grads)
                grad_scores = (probs * slopes).astype(BF)
                dkv_s[first : first + bk, :] += dot_nn(probs.astype(BF), plain) + dot_nn(grad_scores, queries)
                total = total + dot_nn(kt_s[:, first : first + bk], grad_scores)
            dq_s[:, cols] = total
            return 0

        lax.fori_loop(0, steps, main, 0)
        for first in range(0, tokens, step):
            turned = dq_s[:, first : first + step]
            v_s[first : first + step, :] = (
                jnp.concatenate([turned, turned], axis=0).T * scale
            ).astype(BF)

        def spread_band(band, _):
            rows = pl.ds(pl.multiple_of(band * own, 16), own)
            joint = swap_halves(dkv_s[rows, :])
            out_ref[band, :band_tokens] = uncrop(jnp.where(low, joint * scale, joint), width, side).astype(BF)
            pairs = pack_pairs(v_s[rows, :].astype(F32), lanes)
            out_ref[band, band_tokens:] = uncrop(pairs, width, side).astype(BF)
            return 0

        lax.fori_loop(0, used, spread_band, 0)
        if used < bands:
            out_ref[used:] = jnp.zeros((bands - used,) + out_ref.shape[1:], BF)

    for side in (width, width * 3 // 4, width // 2):
        pl.when(side_now == side)(partial(variant, side))


def attend_back(side, qkv, grads, spot, norms, kept, width, scale):
    bands, packed, _ = qkv.shape
    tokens = bands * packed * 2 // 3
    vm = pl.BlockSpec(memory_space=pltpu.VMEM)
    rows = pltpu.VMEM((tokens, 128), BF)
    return pl.pallas_call(
        partial(attend_back_kernel, width, scale),
        out_shape=jax.ShapeDtypeStruct((bands, packed, 128), BF),
        grid=(1,),
        in_specs=[
            pl.BlockSpec(memory_space=pltpu.SMEM),
            vm,
            pl.BlockSpec((1,) + grads.shape[1:], lambda at: (spot, 0, 0, 0)),
            vm,
            pl.BlockSpec(memory_space=pl.ANY),
        ],
        out_specs=vm,
        scratch_shapes=[rows] * 5
        + [
            pltpu.VMEM((64, tokens), BF),
            pltpu.VMEM((64, tokens), F32),
            pltpu.VMEM((tokens, 128), F32),
            pltpu.VMEM((8, tokens), F32),
            pltpu.VMEM((2 * tokens, 1024), BF),
            pltpu.SemaphoreType.DMA((3, 4)),
        ],
        compiler_params=pltpu.CompilerParams(vmem_limit_bytes=62 << 20),
        cost_estimate=pl.CostEstimate(
            flops=8 * 256 * tokens * tokens, bytes_accessed=40 << 20, transcendentals=0
        ),
        name="attend_back",
    )(side, qkv, grads, norms, kept)


def dot_tn(lhs, rhs):
    return lax.dot_general(lhs, rhs, (((0,), (0,)), ((), ())), preferred_element_type=F32)


def row_of(table, at):
    ids = lax.broadcasted_iota(jnp.int32, table.shape, 0)
    return jnp.sum(jnp.where(ids == at, table, 0.0), axis=0, keepdims=True)


def put_row(table_ref, at, row):
    ids = lax.broadcasted_iota(jnp.int32, table_ref.shape, 0)
    table_ref[...] = jnp.where(ids == at, row, table_ref[...])


def col_sum(field):
    return jnp.sum(field, axis=0, keepdims=True)


def vec(ref):
    return ref[...].astype(F32).reshape(1, -1)


def spread_lanes(tile, channels):
    return jnp.concatenate([tile] * (channels // 128), axis=1)


def token_ids(shape):
    return lax.broadcasted_iota(jnp.int32, (shape[0], 128), 0)


def pixel_inside(shape, first_row, side, width):
    token = token_ids(shape)
    row = first_row + lax.shift_right_logical(token, int(math.log2(width)))
    return spread_lanes((row >= 0) & (row < side) & ((token & (width - 1)) < side), shape[1])


def sigmoid(field):
    return 0.5 * jnp.tanh(0.5 * field) + 0.5


def moments(avg_ref, at):
    table = avg_ref[...]
    mean = row_of(table, 2 * at)
    return mean, lax.rsqrt(row_of(table, 2 * at + 1) - mean * mean + GN_EPS)


def put_taps(taps_s, first, field, width, flipped):
    channels = field.shape[1]
    column = token_ids(field.shape) & (width - 1)
    count = field.shape[0]
    left = jnp.where(spread_lanes(column == 0, channels), 0.0, pltpu.roll(field, 1, 0))
    right = jnp.where(spread_lanes(column == width - 1, channels), 0.0, pltpu.roll(field, count - 1, 0))
    order = (right, field, left) if flipped else (left, field, right)
    for at, part in enumerate(order):
        taps_s[first : first + count, at * channels : (at + 1) * channels] = part.astype(BF)


VMEM_WHOLE = pl.BlockSpec(memory_space=pltpu.VMEM)
SMEM_WHOLE = pl.BlockSpec(memory_space=pltpu.SMEM)


def image_block(tokens, channels):
    return pl.BlockSpec((1, tokens, channels), lambda at: (at, 0, 0))


def edge_block(width, channels):
    return pl.BlockSpec((2, 1, width, channels), lambda at: (0, at, 0, 0))


def table_block(channels, rows=8):
    return pl.BlockSpec((rows, channels), lambda at: (0, 0))


def vector_block(channels):
    return pl.BlockSpec((channels,), lambda at: (0,))


def fixed_block(shape):
    return pl.BlockSpec(shape, lambda at: (0,) * len(shape), pipeline_mode=pl.Buffered(1))


def greet_rows(me, bands):
    barrier = pltpu.get_barrier_semaphore()
    for away in range(1, bands):
        pl.semaphore_signal(
            barrier, inc=1, device_id={"rows": lax.rem(me + away, bands)},
            device_id_type=pl.DeviceIdType.MESH,
        )


def meet_rows(bands):
    pl.semaphore_wait(pltpu.get_barrier_semaphore(), bands - 1)


def row_copy(src, dst, send, recv, target):
    return pltpu.make_async_remote_copy(
        src_ref=src, dst_ref=dst, send_sem=send, recv_sem=recv, device_id={"rows": target},
        device_id_type=pl.DeviceIdType.MESH,
    )


def edge_copies(top, bottom, halo, at, send, recv, me, bands):
    return [
        row_copy(top, halo.at[1, at], send.at[0, at], recv.at[1, at], lax.rem(me + bands - 1, bands)),
        row_copy(bottom, halo.at[0, at], send.at[1, at], recv.at[0, at], lax.rem(me + 1, bands)),
    ]


def group_average(sums, weight_ref, sides, slots, send, recv, me, bands):
    slots[me] = sums
    copies = [
        row_copy(slots.at[me], slots.at[me], send.at[away], recv.at[me], lax.rem(me + away, bands))
        for away in range(1, bands)
    ]
    for item in copies:
        item.start()
    for away in range(1, bands):
        source = lax.rem(me + away, bands)
        row_copy(slots.at[source], slots.at[source], send.at[away], recv.at[source], source).wait_recv()
    total = slots[0]
    for at in range(1, bands):
        total = total + slots[at]
    for item in copies:
        item.wait_send()
    if weight_ref is not None:
        total = total * vec(weight_ref)
    image = lax.shift_right_logical(lax.broadcasted_iota(jnp.int32, total.shape, 0), 1)
    side = jnp.ones(total.shape, jnp.int32)
    for at in range(sides.shape[0]):
        side = jnp.where(image == at, sides[at], side)
    side = side.astype(F32)
    channels = total.shape[1]
    size = channels // GROUPS
    lane = lax.broadcasted_iota(jnp.int32, total.shape, 1)
    step = 1
    while step < size:
        total = total + jnp.where(
            (lane & step) == 0, pltpu.roll(total, channels - step, 1), pltpu.roll(total, step, 1)
        )
        step *= 2
    return total / (side * side * size)


def exchange_scratch(images, width, channels, bands):
    return [
        pltpu.VMEM((2, images, width, channels), BF),
        pltpu.VMEM((bands, 8, channels), F32),
        pltpu.SemaphoreType.DMA((2, images)),
        pltpu.SemaphoreType.DMA((2, images)),
        pltpu.SemaphoreType.DMA((bands,)),
        pltpu.SemaphoreType.DMA((bands,)),
    ]


def share_edges(grads, at, width, halo_ref, scratch, me, bands, met=False):
    edge_s, _, send, recv = scratch[:4]
    tokens = grads.shape[0]
    edge_s[0, at] = grads[:width].astype(BF)
    edge_s[1, at] = grads[tokens - width :].astype(BF)
    if not met:
        pl.when(at == 0)(partial(meet_rows, bands))
    for item in edge_copies(edge_s.at[0, at], edge_s.at[1, at], halo_ref, at, send, recv, me, bands):
        item.start()


def close_exchange(sums, weight_ref, sides, avg_ref, halo_ref, scratch, me, bands):
    edge_s, slots, send, recv, sum_send, sum_recv = scratch
    avg_ref[...] = group_average(sums, weight_ref, sides, slots, sum_send, sum_recv, me, bands)
    for at in range(edge_s.shape[1]):
        for item in edge_copies(
            edge_s.at[0, at], edge_s.at[1, at], halo_ref, at, send, recv, me, bands
        ):
            item.wait_send()
        for end in range(2):
            edge = halo_ref.at[end, at]
            row_copy(
                edge, edge, send.at[end, at], recv.at[end, at], lax.rem(me + 1, bands)
            ).wait_recv()


def begin_kernel(width, bands, place, sides, field_ref, whole_ref, avg_ref, halo_ref, sums_s, slots, send, recv, sum_send, sum_recv):
    at = pl.program_id(0)
    last = pl.num_programs(0) - 1
    me = lax.axis_index("rows")
    images, tokens, _ = whole_ref.shape

    def edges():
        return [
            edge_copies(
                whole_ref.at[image, pl.ds(0, width)], whole_ref.at[image, pl.ds(tokens - width, width)],
                halo_ref, image, send, recv, me, bands,
            )
            for image in range(images)
        ]

    @pl.when(at == 0)
    def _():
        greet_rows(me, bands)
        sums_s[...] = jnp.zeros_like(sums_s)

    @pl.when(at == 1)
    def _():
        meet_rows(bands)
        for pair in edges():
            for item in pair:
                item.start()

    field = field_ref[0].astype(F32)
    field = jnp.where(pixel_inside(field.shape, place[0], sides[at], width), field, 0.0)
    put_row(sums_s, 2 * at, col_sum(field))
    put_row(sums_s, 2 * at + 1, col_sum(field * field))

    @pl.when(at == last)
    def _():
        avg_ref[...] = group_average(
            sums_s[...], None, sides, slots, sum_send, sum_recv, me, bands
        )
        for image, pair in enumerate(edges()):
            for item in pair:
                item.wait_send()
            for end in range(2):
                edge = halo_ref.at[end, image]
                row_copy(
                    edge, edge, send.at[end, image], recv.at[end, image], lax.rem(me + 1, bands)
                ).wait_recv()


def begin(place, sides, field, width, bands):
    images, tokens, channels = field.shape
    anywhere = pl.BlockSpec(memory_space=pl.ANY)
    return pl.pallas_call(
        partial(begin_kernel, width, bands),
        grid=(images,),
        out_shape=(
            jax.ShapeDtypeStruct((8, channels), F32),
            jax.ShapeDtypeStruct((2, images, width, channels), BF),
        ),
        in_specs=[
            SMEM_WHOLE,
            SMEM_WHOLE,
            image_block(tokens, channels),
            anywhere,
        ],
        out_specs=(table_block(channels), anywhere),
        scratch_shapes=[pltpu.VMEM((8, channels), F32)]
        + exchange_scratch(images, width, channels, bands)[1:],
        compiler_params=pltpu.CompilerParams(collective_id=1, has_side_effects=True),
        name="begin",
    )(place, sides, field, field)


def conv_forward_kernel(width, bands, base_given, *refs):
    place, sides, field_ref, halo_ref, avg_ref, gain_ref, bias_ref, weight_ref, shift_ref = refs[:9]
    refs = refs[9:]
    if base_given:
        base_ref, refs = refs[0], refs[1:]
    out_ref, next_avg, next_halo = refs[:3]
    refs = refs[3:]
    taps_s, stats_ref = refs[:2]
    scratch = refs[2:]
    me = lax.axis_index("rows")
    at = pl.program_id(0)
    last = pl.num_programs(0) - 1

    @pl.when(at == 0)
    def _():
        greet_rows(me, bands)
        stats_ref[...] = jnp.zeros_like(stats_ref)

    _, tokens, channels = field_ref.shape
    first_row = place[0]
    side = sides[at]
    mean, inv_std = moments(avg_ref, at)
    slope = inv_std * vec(gain_ref)
    offset = vec(bias_ref) - mean * slope

    def active(field, row):
        normed = field.astype(F32) * slope + offset
        inside = pixel_inside(normed.shape, row, side, width)
        return jnp.where(inside, normed * sigmoid(normed), 0.0)

    rows = tokens // width
    put_taps(taps_s, 0, active(halo_ref[0, 0], first_row - 1), width, False)
    put_taps(taps_s, width, active(field_ref[0], first_row), width, False)
    put_taps(taps_s, width + tokens, active(halo_ref[1, 0], first_row + rows), width, False)
    deep = 3 * channels
    total = dot_nn(taps_s[:tokens], weight_ref[:deep])
    for tap in (1, 2):
        total = total + dot_nn(
            taps_s[tap * width : tap * width + tokens], weight_ref[tap * deep : (tap + 1) * deep]
        )
    total = total + row_of(shift_ref[...], at)
    inside = pixel_inside(total.shape, first_row, side, width)
    if base_given:
        total = total + jnp.where(inside, base_ref[0].astype(F32), 0.0)
    out_ref[0] = total
    share_edges(total, at, width, next_halo, scratch, me, bands)
    masked = jnp.where(inside, total, 0.0)
    put_row(stats_ref, 2 * at, col_sum(masked))
    put_row(stats_ref, 2 * at + 1, col_sum(masked * masked))

    @pl.when(at == last)
    def _():
        close_exchange(stats_ref[...], None, sides, next_avg, next_halo, scratch, me, bands)


def conv_forward(place, sides, field, halo, avg, gain, bias, weight, shift, base, width, bands):
    images, tokens, channels = field.shape
    added = base is not None
    tok = image_block(tokens, channels)
    return pl.pallas_call(
        partial(conv_forward_kernel, width, bands, added),
        grid=(images,),
        out_shape=(
            jax.ShapeDtypeStruct(field.shape, F32),
            jax.ShapeDtypeStruct((8, channels), F32),
            jax.ShapeDtypeStruct((2, images, width, channels), BF),
        ),
        in_specs=[
            SMEM_WHOLE,
            SMEM_WHOLE,
            tok,
            edge_block(width, channels),
            table_block(channels),
            vector_block(channels),
            vector_block(channels),
            fixed_block(weight.shape),
            table_block(channels),
        ]
        + ([tok] if added else []),
        out_specs=(tok, table_block(channels), pl.BlockSpec(memory_space=pl.ANY)),
        scratch_shapes=[
            pltpu.VMEM((tokens + 2 * width, 3 * channels), BF),
            pltpu.VMEM((8, channels), F32),
        ]
        + exchange_scratch(images, width, channels, bands),
        compiler_params=pltpu.CompilerParams(
            vmem_limit_bytes=62 << 20, collective_id=2 if added else 3, has_side_effects=True
        ),
        name="conv_forward",
    )(place, sides, field, halo, avg, gain, bias, weight, shift, *([base] if added else []))


class BandFold:
    def __init__(self, parts, scratch, me):
        self.parts, self.me = parts, me
        count = len(parts)
        self.own, self.pair, self.first, self.second_s = (
            scratch[at * count : (at + 1) * count] for at in range(4)
        )
        self.load, self.pair_send, self.pair_recv, self.hop_send, self.hop_recv = scratch[4 * count :]
        self.core, self.chip = lax.rem(me, 2), me // 2
        self.chunks = fold_chunks([part.shape for part in parts])

    def loads(self, which):
        size = self.parts[which].shape[0] // 8
        return [
            pltpu.make_async_copy(
                self.parts[which].at[pl.ds(pl.multiple_of((2 * spot + self.core) * size, 16), size)],
                self.own[which].at[spot],
                self.load.at[which, spot],
            )
            for spot in range(4)
        ]

    def pairs(self, which):
        size = self.parts[which].shape[0] // 8
        return [
            row_copy(
                self.parts[which].at[pl.ds(pl.multiple_of((2 * spot + 1 - self.core) * size, 16), size)],
                self.pair[which].at[spot],
                self.pair_send.at[which, spot],
                self.pair_recv.at[which, spot],
                self.me + 1 - 2 * self.core,
            )
            for spot in range(4)
        ]

    def hops(self, at):
        which, first, wide, one, two = self.chunks[at]
        cols = pl.ds(first, wide)
        near, far = jnp.bitwise_xor(self.chip, one), jnp.bitwise_xor(self.chip, two)

        def hop(spot, dst, step, chip):
            return row_copy(
                self.own[which].at[spot, :, cols], dst, self.hop_send.at[at, step], self.hop_recv.at[at, step],
                2 * chip + self.core,
            )

        return [
            hop(near, self.first[which].at[0, :, cols], 0, near),
            hop(jnp.bitwise_xor(near, two), self.first[which].at[1, :, cols], 1, near),
            hop(far, self.second_s[which].at[:, cols], 2, far),
        ]

    def start(self):
        for which in range(len(self.parts)):
            for item in self.loads(which) + self.pairs(which):
                item.start()

    def spread(self):
        for which in range(len(self.parts)):
            for item in self.loads(which):
                item.wait()
            for item in self.pairs(which):
                item.wait_recv()
            for spot in range(4):
                self.own[which][spot] = self.own[which][spot] + self.pair[which][spot]
        for at in range(len(self.chunks)):
            for item in self.hops(at)[:2]:
                item.start()

    def second(self):
        for at, (which, first, wide, _, two) in enumerate(self.chunks):
            cols = pl.ds(first, wide)
            for step, item in enumerate(self.hops(at)[:2]):
                item.wait()
                spot = jnp.bitwise_xor(self.chip, two) if step else self.chip
                self.own[which][spot, :, cols] = (
                    self.own[which][spot, :, cols] + self.first[which][step, :, cols]
                )
            self.hops(at)[2].start()

    def finish(self, outs):
        for at, (which, first, wide, _, _) in enumerate(self.chunks):
            cols = pl.ds(first, wide)
            self.hops(at)[2].wait()
            outs[which][:, cols] = self.own[which][self.chip, :, cols] + self.second_s[which][:, cols]
        for which in range(len(self.parts)):
            for item in self.pairs(which):
                item.wait_send()


def fold_chunks(shapes):
    total = sum(rows * cols for rows, cols in shapes)
    rows, cols = shapes[0]
    wide = (total // 2 // rows + 64) // 128 * 128
    chunks = [(0, 0, wide, 1, 2), (0, wide, cols - wide, 2, 1)]
    return chunks + [(at, 0, shape[1], 2, 1) for at, shape in enumerate(shapes) if at]


def fold_scratch(shapes):
    def bufs(lead):
        return [pltpu.VMEM(lead + (rows // 8, cols), BF) for rows, cols in shapes]

    chunks = len(fold_chunks(shapes))
    return (
        bufs((4,)) + bufs((4,)) + bufs((2,)) + bufs(())
        + [pltpu.SemaphoreType.DMA((len(shapes), 4))] * 3
        + [pltpu.SemaphoreType.DMA((chunks, 3))] * 2
    )


class GroupTree:
    def __init__(self, fields, outs, scratch, group):
        self.fields, self.outs, self.group = fields, outs, group
        count = len(fields)
        self.near_s, self.far_s = scratch[:count], scratch[count : 2 * count]
        self.send, self.recv = scratch[2 * count :]
        self.odd = lax.rem(group, 2)

    def half(self, which, odd):
        size = self.fields[which].shape[0] // 2
        return pl.ds(pl.multiple_of(odd * size, 16), size)

    def copies(self, which, step):
        mine, theirs = self.half(which, self.odd), self.half(which, 1 - self.odd)
        out = self.outs[which].at[mine]
        src, dst, bit = (
            (self.fields[which].at[theirs], self.near_s[which], 1),
            (self.fields[which].at[mine], self.far_s[which], 2),
            (out, out, 1),
        )[step]
        return pltpu.make_async_remote_copy(
            src_ref=src, dst_ref=dst, send_sem=self.send.at[which, step], recv_sem=self.recv.at[which, step],
            device_id={"heads": jnp.bitwise_xor(self.group, bit)}, device_id_type=pl.DeviceIdType.MESH,
        )

    def near(self):
        for which in range(len(self.fields)):
            self.copies(which, 0).start()

    def far(self):
        for which in range(len(self.fields)):
            mine = self.half(which, self.odd)
            self.copies(which, 0).wait()
            self.fields[which][mine] = (
                self.fields[which][mine].astype(F32) + self.near_s[which][...].astype(F32)
            ).astype(BF)
            self.copies(which, 1).start()

    def back(self):
        for which in range(len(self.fields)):
            mine = self.half(which, self.odd)
            self.copies(which, 1).wait()
            self.outs[which][mine] = (
                self.fields[which][mine].astype(F32) + self.far_s[which][...].astype(F32)
            ).astype(BF)
            self.copies(which, 2).start()

    def end(self):
        for which in range(len(self.fields)):
            self.copies(which, 2).wait_send()
            theirs = self.outs[which].at[self.half(which, 1 - self.odd)]
            pltpu.make_async_remote_copy(
                src_ref=theirs, dst_ref=theirs, send_sem=self.send.at[which, 2],
                recv_sem=self.recv.at[which, 2], device_id={"heads": jnp.bitwise_xor(self.group, 1)},
                device_id_type=pl.DeviceIdType.MESH,
            ).wait_recv()


def tree_scratch(shapes):
    return [pltpu.VMEM((rows // 2, cols), BF) for rows, cols in shapes] * 2 + [
        pltpu.SemaphoreType.DMA((len(shapes), 3))
    ] * 2


def conv_backward_kernel(width, bands, added, late, summed, *refs):
    refs = list(refs)
    late_refs, refs = refs[:late], refs[late:]
    summed_refs, refs = refs[:summed], refs[summed:]
    me = lax.axis_index("rows")
    (place, sides, grad_ref, grad_halo, field_ref, field_halo, avg_ref, back_avg, gain_ref) = refs[:9]
    refs = refs[9:]
    if added:
        add_ref, add_halo = refs[:2]
        refs = refs[2:]
    (weight_ref, prior_ref, prior_avg, prior_gain, prior_bias) = refs[:5]
    refs = refs[5:]
    late_outs, refs = refs[:late], refs[late:]
    summed_outs, refs = refs[:summed], refs[summed:]
    if added:
        kept_ref = refs[0]
        refs = refs[1:]
    out_ref, next_avg, stats_ref, sums_ref, weight_grad = refs[:5]
    next_halo = None
    if added:
        next_halo = refs[5]
        refs = refs[1:]
    taps_s, act_s, total_s = refs[5:8]
    scratch = refs[8:]
    if late:
        base = 6 if added else 3
        after = base + 4 * late + 5
        fold = BandFold(late_refs, scratch[base:after], me)
        if summed:
            fields, made = scratch[after : after + summed], scratch[after + summed : after + 2 * summed]
            group = lax.axis_index("heads")
            tree = GroupTree(fields, made, scratch[after + 2 * summed :], group)
        scratch = scratch[:base]
    at = pl.program_id(0)
    last = pl.num_programs(0) - 1
    _, tokens, channels = grad_ref.shape
    first_row = place[0]
    side = sides[at]
    mean, inv_std = moments(avg_ref, at)
    back = back_avg[...]
    back_mean, back_cross = row_of(back, 2 * at), row_of(back, 2 * at + 1)
    gain = vec(gain_ref)
    grad_slope = inv_std * gain
    field_slope = inv_std * inv_std * back_cross
    offset = inv_std * back_mean - mean * field_slope

    def through(grads, field, extra, row):
        moved = grads.astype(F32) * grad_slope - field.astype(F32) * field_slope - offset
        if extra is not None:
            moved = moved + extra.astype(F32)
        return jnp.where(pixel_inside(moved.shape, row, side, width), moved, 0.0)

    rows = tokens // width
    own = through(grad_ref[0], field_ref[0], add_ref[0] if added else None, first_row)
    put_taps(taps_s, width, own, width, True)
    for end, row, first in ((0, first_row - 1, 0), (1, first_row + rows, width + tokens)):
        put_taps(
            taps_s,
            first,
            through(grad_halo[end, 0], field_halo[end, 0], add_halo[end, 0] if added else None, row),
            width,
            True,
        )
    if added:
        kept_ref[0] = own

    @pl.when(at == 0)
    def _():
        greet_rows(me, bands)
        stats_ref[...] = jnp.zeros_like(stats_ref)
        sums_ref[...] = jnp.zeros_like(sums_ref)
        if summed:
            for bit in (1, 2):
                pl.semaphore_signal(
                    pltpu.get_barrier_semaphore(), inc=1, device_id={"heads": jnp.bitwise_xor(group, bit)},
                    device_id_type=pl.DeviceIdType.MESH,
                )
            for field, ref in zip(fields, summed_refs):
                field[...] = ref[...]
        if late:
            meet_rows(bands + 2 if summed else bands)
            fold.start()
        if summed:
            tree.near()
        total_s[...] = jnp.zeros_like(total_s)

    put_row(sums_ref, at, col_sum(own))
    prior_mean, prior_std = moments(prior_avg, at)
    centred = (prior_ref[0].astype(F32) - prior_mean) * prior_std
    normed = centred * vec(prior_gain) + vec(prior_bias)
    gate = sigmoid(normed)
    inside = pixel_inside(normed.shape, first_row, side, width)
    act_s[...] = jnp.where(inside, normed * gate, 0.0).astype(BF).T
    act_t = act_s[...]
    moved = None
    for down in range(3):
        lines = pl.ds((2 - down) * width, tokens)
        for across in range(3):
            tap = 3 * down + across
            low = taps_s[lines, across * channels : (across + 1) * channels]
            part = slice(tap * channels, (tap + 1) * channels)
            term = dot_nt(low, weight_ref[part])
            moved = term if moved is None else moved + term
            total_s[part] += dot_nn(act_t, low)
    if late:
        pl.when(at == 0)(fold.spread)
        pl.when(at == 2)(fold.second)
    if summed:
        pl.when(at == 1)(tree.far)
        pl.when(at == 2)(tree.back)
    grads = jnp.where(inside, moved * (gate + normed * gate * (1.0 - gate)), 0.0)
    out_ref[0] = grads
    if added:
        share_edges(grads, at, width, next_halo, scratch, me, bands, late > 0)
    put_row(stats_ref, 2 * at, col_sum(grads))
    put_row(stats_ref, 2 * at + 1, col_sum(grads * centred))

    @pl.when(at == last)
    def _():
        if late:
            fold.finish(late_outs)
        if summed:
            tree.end()
            for out, field in zip(summed_outs, made):
                out[...] = field[...]
        if added:
            close_exchange(stats_ref[...], prior_gain, sides, next_avg, next_halo, scratch, me, bands)
        else:
            if not late:
                meet_rows(bands)
            next_avg[...] = group_average(stats_ref[...], prior_gain, sides, *scratch, me, bands)
        weight_grad[...] = total_s[...].astype(BF)


def conv_backward(place, sides, grads, grad_halo, field, field_halo, avg, back_avg, gain, extra,
                  extra_halo, weight, prior, prior_avg, prior_gain, prior_bias, late, summed, width, bands):
    images, tokens, channels = grads.shape
    added = extra is not None
    tok = image_block(tokens, channels)
    edge = edge_block(width, channels)
    table = table_block(channels)
    vector = vector_block(channels)
    anywhere = pl.BlockSpec(memory_space=pl.ANY)
    ins = [*late, *summed, place, sides, grads, grad_halo, field, field_halo, avg, back_avg, gain]
    specs = [anywhere] * len(late) + [fixed_block(part.shape) for part in summed] + [SMEM_WHOLE, SMEM_WHOLE, tok, edge, tok, edge, table, table, vector]
    if added:
        ins += [extra, extra_halo]
        specs += [tok, edge]
    ins += [weight, prior, prior_avg, prior_gain, prior_bias]
    specs += [fixed_block(weight.shape), tok, table, vector, vector]
    outs = [
        jax.ShapeDtypeStruct(grads.shape, F32),
        jax.ShapeDtypeStruct((8, channels), F32),
        jax.ShapeDtypeStruct((8, channels), F32),
        jax.ShapeDtypeStruct((8, channels), F32),
        jax.ShapeDtypeStruct(weight.shape, BF),
    ]
    out_specs = [tok, table, table, table, fixed_block(weight.shape)]
    if added:
        outs.append(jax.ShapeDtypeStruct((2, images, width, channels), BF))
        out_specs.append(pl.BlockSpec(memory_space=pl.ANY))
        outs.insert(0, jax.ShapeDtypeStruct(grads.shape, F32))
        out_specs.insert(0, tok)
    shapes = [(part.shape[0] // 8, part.shape[1]) for part in late] + [part.shape for part in summed]
    outs = [jax.ShapeDtypeStruct(shape, BF) for shape in shapes] + outs
    out_specs = [fixed_block(shape) for shape in shapes] + out_specs
    return pl.pallas_call(
        partial(conv_backward_kernel, width, bands, added, len(late), len(summed)),
        grid=(images,),
        out_shape=outs,
        in_specs=specs,
        out_specs=out_specs,
        scratch_shapes=[
            pltpu.VMEM((tokens + 2 * width, 3 * channels), BF),
            pltpu.VMEM((channels, tokens), BF),
            pltpu.VMEM(weight.shape, F32),
        ]
        + (
            exchange_scratch(images, width, channels, bands)
            if added
            else [
                pltpu.VMEM((bands, 8, channels), F32),
                pltpu.SemaphoreType.DMA((bands,)),
                pltpu.SemaphoreType.DMA((bands,)),
            ]
        )
        + (fold_scratch([part.shape for part in late]) if late else [])
        + [pltpu.VMEM(part.shape, BF) for part in (*summed, *summed)]
        + (tree_scratch([part.shape for part in summed]) if summed else []),
        compiler_params=pltpu.CompilerParams(
            vmem_limit_bytes=62 << 20, collective_id=4 if added else 6, has_side_effects=True
        ),
        name="conv_backward",
    )(*ins)


def layer_stats(field):
    centre = jnp.mean(field, axis=-1, keepdims=True)
    centred = field - centre
    inv_std = lax.rsqrt(jnp.mean(centred * centred, axis=-1, keepdims=True) + LN_EPS)
    return centred * inv_std, inv_std


def layer_back(grads, gain, centred, inv_std):
    scaled = grads * gain
    return inv_std * (
        scaled
        - jnp.mean(scaled, axis=-1, keepdims=True)
        - centred * jnp.mean(scaled * centred, axis=-1, keepdims=True)
    )


def turn_qkv(weight_ref, turned_s):
    rows, channels = weight_ref.shape[0], weight_ref.shape[1] // 3
    low = lane_ids(rows) < 64
    for head in range(HEADS):
        first = (head // 2) * 128
        keys = weight_ref[:, channels + first : channels + first + 128].astype(F32)
        values = weight_ref[:, 2 * channels + first : 2 * channels + first + 128].astype(F32)
        if head % 2 == 0:
            joint = jnp.where(low, keys, swap_halves(values))
        else:
            joint = jnp.where(low, swap_halves(keys), values)
        turned_s[:, head * 128 : head * 128 + 128] = joint.astype(BF)
    turned_s[:, 2 * channels :] = weight_ref[:, :channels]


def entry_kernel(bands, direct, field_ref, avg_ref, gain_ref, bias_ref, proj_ref, proj_bias, ln_gain,
                 ln_bias, qkv_ref, stream_ref, *refs):
    images = pl.num_programs(0)
    at = pl.program_id(0)
    if direct:
        count = len(refs) - 4
        sent_refs, (turned_s, first_s, send, recv) = refs[:count], refs[count:]
        me = lax.axis_index("rows")
    else:
        sent_refs, turned_s = refs[:-1], refs[-1]
    _, tokens, channels = field_ref.shape
    half = tokens // 2

    @pl.when(at == 0)
    def _():
        if direct:
            greet_rows(me, bands)
        turn_qkv(qkv_ref, turned_s)

    mean, inv_std = moments(avg_ref, at)
    slope = inv_std * vec(gain_ref)
    flat = (field_ref[0] * slope + (vec(bias_ref) - mean * slope)).astype(BF)
    stream = dot_nn(flat, proj_ref[...]) + vec(proj_bias)
    stream_ref[0] = stream
    centred, _ = layer_stats(stream)
    joint = dot_nn((centred * vec(ln_gain) + vec(ln_bias)).astype(BF), turned_s[...])
    low = lane_ids(half) < 64

    def put(out):
        for head in range(HEADS):
            out[head, :tokens] = joint[:, head * 128 : head * 128 + 128].astype(BF)
            first = 2 * channels + (head // 2) * 128
            upper, lower = joint[:half, first : first + 128], joint[half:, first : first + 128]
            if head % 2 == 0:
                pairs = jnp.where(low, upper, swap_halves(lower))
            else:
                pairs = jnp.where(low, swap_halves(upper), lower)
            out[head, tokens:] = pairs.astype(BF)

    for image, out in enumerate(sent_refs):
        pl.when(at == image)(partial(put, first_s if direct and image == 0 else out))
    if not direct:
        return
    copies = [
        row_copy(
            first_s.at[lax.rem(me + away, bands)], sent_refs[0].at[me], send.at[away], recv.at[me],
            lax.rem(me + away, bands),
        )
        for away in range(1, bands)
    ]
    own = pltpu.make_async_copy(first_s.at[me], sent_refs[0].at[me], recv.at[me])

    @pl.when(at == 0)
    def _():
        meet_rows(bands)
        for item in copies:
            item.start()
        own.start()

    @pl.when(at == images - 1)
    def _():
        own.wait()
        for away, item in enumerate(copies):
            item.wait_send()
            source = lax.rem(me + away + 1, bands)
            row_copy(
                sent_refs[0].at[source], sent_refs[0].at[source], send.at[away + 1], recv.at[source], source
            ).wait_recv()


def entry(field, avg, gain, bias, proj, proj_bias, ln_gain, ln_bias, qkv, bands):
    images, tokens, channels = field.shape
    vector = vector_block(channels)
    direct = bands == HEADS
    packed = (HEADS, tokens * 3 // 2, 128)
    anywhere = pl.BlockSpec(memory_space=pl.ANY)
    params = {"collective_id": 9, "has_side_effects": True} if direct else {}
    return pl.pallas_call(
        partial(entry_kernel, bands, direct),
        grid=(images,),
        out_shape=(jax.ShapeDtypeStruct(field.shape, F32),)
        + (jax.ShapeDtypeStruct(packed, BF),) * images,
        in_specs=[
            image_block(tokens, channels),
            table_block(channels),
            vector,
            vector,
            fixed_block(proj.shape),
            vector,
            vector,
            vector,
            fixed_block(qkv.shape),
        ],
        out_specs=(image_block(tokens, channels),)
        + ((anywhere,) if direct else (fixed_block(packed),))
        + (fixed_block(packed),) * (images - 1),
        scratch_shapes=[pltpu.VMEM(qkv.shape, BF)]
        + (
            [
                pltpu.VMEM(packed, BF),
                pltpu.SemaphoreType.DMA((bands,)),
                pltpu.SemaphoreType.DMA((bands,)),
            ]
            if direct
            else []
        ),
        compiler_params=pltpu.CompilerParams(vmem_limit_bytes=62 << 20, **params),
        name="entry",
    )(field, avg, gain, bias, proj, proj_bias, ln_gain, ln_bias, qkv)


def join_heads(pairs_ref, at):
    half = pairs_ref.shape[-2]
    low = lane_ids(half) < 64
    upper, lower = [], []
    for head in range(0, HEADS, 2):
        one, two = pairs_ref[at, head].astype(F32), pairs_ref[at, head + 1].astype(F32)
        upper.append(jnp.where(low, one, swap_halves(two)))
        lower.append(jnp.where(low, swap_halves(one), two))
    return jnp.concatenate(
        [jnp.concatenate(upper, axis=1), jnp.concatenate(lower, axis=1)], axis=0
    ).astype(BF)


def split_heads(field, out_ref, at):
    half = field.shape[0] // 2
    low = lane_ids(half) < 64
    for head in range(HEADS):
        first = (head // 2) * 128
        upper, lower = field[:half, first : first + 128], field[half:, first : first + 128]
        if head % 2 == 0:
            pairs = jnp.where(low, upper, swap_halves(lower))
        else:
            pairs = jnp.where(low, swap_halves(upper), lower)
        out_ref[at, head] = pairs.astype(BF)


def feed_pieces(channels, wide, hidden, bands):
    size = channels // bands
    geglu = [(at * size, size) for at in range(wide // channels)]
    first = wide // bands
    return (
        geglu,
        [(first, hidden // bands)],
        [(first + hidden // bands, size)],
        [(first + hidden // bands + size, size)],
    )


def feed_kernel(width, bands, per_band, halving, place, sides, *refs):
    given, refs = refs[:per_band], refs[per_band:]
    cot_hbm, refs = refs[0], refs[1:]
    count = 4 if halving else 1
    grads_ref, refs = refs[18 : 18 + count], refs[:18] + refs[18 + count :]
    (stream_ref, residual_ref, cot_ref, cross_ref, attn_ref, attn_bias, ln_gain, ln_bias,
     geglu_hbm, geglu_bias, feed_hbm, feed_bias, proj_ref, proj_bias,
     out_ref, three_ref, back_ref, ride_halo, sums_ref, cross_sum, pair_sums, geglu_s, feed_s, proj_s, attn_s,
     geglu_ref, feed_ref, weight_sems, ride_send, ride_recv, turned_s, mixed_s, sent_s, out_send, out_recv, back_send, back_recv, *more) = refs
    if halving:
        given_s, taken_s, pair_sems = more
    at = pl.program_id(0)
    images = pl.num_programs(0)
    last = images - 1
    me = lax.axis_index("rows")

    def move(src, dst, send, recv, target):
        @pl.when(target != me)
        def _():
            pltpu.make_async_remote_copy(
                src_ref=src, dst_ref=dst, send_sem=send, recv_sem=recv, device_id={"rows": target},
                device_id_type=pl.DeviceIdType.MESH,
            ).start()

        @pl.when(target == me)
        def _():
            pltpu.make_async_copy(src, dst, recv).start()

    def arrived(dst, send, recv, source):
        @pl.when(source != me)
        def _():
            pltpu.make_async_remote_copy(
                src_ref=dst, dst_ref=dst, send_sem=send, recv_sem=recv, device_id={"rows": source},
                device_id_type=pl.DeviceIdType.MESH,
            ).wait_recv()

        @pl.when(source == me)
        def _():
            pltpu.make_async_copy(dst, dst, recv).wait()

    def left(src, send, recv, target):
        @pl.when(target != me)
        def _():
            pltpu.make_async_remote_copy(
                src_ref=src, dst_ref=src, send_sem=send, recv_sem=recv, device_id={"rows": target},
                device_id_type=pl.DeviceIdType.MESH,
            ).wait_send()

    def send_spot(spot):
        item = me * per_band + spot
        head, image = item // images, lax.rem(item, images)
        for away in range(bands):
            band = lax.rem(me + away, bands)
            move(
                given[spot].at[band], mixed_s.at[image, head], out_send.at[spot, away],
                out_recv.at[image, head], band,
            )

    loads = [
        pltpu.make_async_copy(src, dst, weight_sems.at[spot])
        for spot, (src, dst) in enumerate(((geglu_hbm, geglu_ref), (feed_hbm, feed_ref)))
    ]

    @pl.when(at == 0)
    def _():
        greet_rows(me, bands)
        meet_rows(bands)
        send_spot(0)
        for item in loads:
            item.start()

    for head in range(HEADS):
        arrived(
            mixed_s.at[at, head], out_send.at[0, 0], out_recv.at[at, head], (head * images + at) // per_band
        )
    @pl.when(at == 0)
    def _():
        for item in loads:
            item.wait()

    def ride(image):
        below = cot_hbm.shape[1] - width
        return edge_copies(
            cot_hbm.at[image, pl.ds(0, width)], cot_hbm.at[image, pl.ds(below, width)], ride_halo, image,
            ride_send, ride_recv, me, bands,
        )

    @pl.when(at == images - 1)
    def _():
        for image in range(sent_s.shape[0]):
            for item in ride(image):
                item.start()

    for spot in range(1, per_band):
        pl.when(at == spot - 1)(partial(send_spot, spot))
    _, tokens, channels = stream_ref.shape
    hidden = feed_ref.shape[0]
    side = sides[at]
    inside = pixel_inside((tokens, channels), place[0], side, width)

    @pl.when(at == 0)
    def _():
        for ref in (sums_ref, cross_sum, pair_sums, geglu_s, feed_s, proj_s, attn_s):
            ref[...] = jnp.zeros_like(ref)

    mixed = join_heads(mixed_s, at)
    three = stream_ref[0] + dot_nn(mixed, attn_ref[...]) + (vec(attn_bias) + row_of(cross_ref[...], at))
    centred, inv_std = layer_stats(three)
    feed_in = (centred * vec(ln_gain) + vec(ln_bias)).astype(BF)
    grad_out = jnp.where(inside, cot_ref[0].astype(F32), 0.0)
    branch = grad_out.astype(BF)
    grad_four = dot_nt(branch, proj_ref[...])
    low_feed = grad_four.astype(BF)
    low_feed_t = low_feed.T
    feed_in_t = feed_in.T
    four = three + vec(feed_bias)
    grad_in = jnp.zeros((tokens, channels), F32)
    step = 512

    pair_bias = vec(geglu_bias)

    def products(first):
        own = slice(first, first + step)
        gates = slice(hidden + first, hidden + first + step)
        value = dot_nn(feed_in, geglu_ref[:, own]) + pair_bias[:, own]
        gate = dot_nn(feed_in, geglu_ref[:, gates]) + pair_bias[:, gates]
        return value, gate, dot_nt(low_feed, feed_ref[own])

    ahead = products(0)
    for first in range(0, hidden, step):
        own = slice(first, first + step)
        gates = slice(hidden + first, hidden + first + step)
        value, gate, back = ahead
        if first + step < hidden:
            ahead = products(first + step)
        below = 0.5 + 0.5 * lax.erf(gate * math.sqrt(0.5))
        bell = jnp.exp(gate * gate * -0.5) * (1.0 / math.sqrt(2.0 * math.pi))
        act = gate * below
        gated = (value * act).astype(BF)
        four = four + dot_nn(gated, feed_ref[own])
        feed_s[:, own] += dot_nn(low_feed_t, gated)
        grad_value = back * act
        grad_gate = back * value * (below + gate * bell)
        pair_sums[:, own] += col_sum(grad_value)
        pair_sums[:, gates] += col_sum(grad_gate)
        low_value, low_gate = grad_value.astype(BF), grad_gate.astype(BF)
        geglu_s[:, own] += dot_nn(feed_in_t, low_value)
        geglu_s[:, gates] += dot_nn(feed_in_t, low_gate)
        grad_in = grad_in + dot_nt(low_value, geglu_ref[:, own]) + dot_nt(low_gate, geglu_ref[:, gates])
    last_in = four.astype(BF)
    proj_s[...] += dot_tn(last_in, branch)
    output = residual_ref[0] + dot_nn(last_in, proj_ref[...]) + vec(proj_bias)
    out_ref[0] = jnp.where(inside, output, 0.0).astype(BF)
    grad_three = grad_four + layer_back(grad_in, vec(ln_gain), centred, inv_std)
    three_ref[0] = grad_three
    low_attn = grad_three.astype(BF)
    attn_s[...] += dot_tn(mixed, low_attn)
    split_heads(dot_nt(low_attn, attn_ref[...]), sent_s, at)
    for head in range(HEADS):
        item = head * images + at
        move(
            sent_s.at[at, head], back_ref.at[lax.rem(item, per_band), me], back_send.at[at, head],
            back_recv.at[lax.rem(item, per_band), me], item // per_band,
        )
    put_row(cross_sum, at, col_sum(grad_three))
    ids = lax.broadcasted_iota(jnp.int32, sums_ref.shape, 0)
    for row, total in enumerate(
        (col_sum(grad_out), col_sum(grad_four), col_sum(grad_in * centred), col_sum(grad_in))
    ):
        sums_ref[...] += jnp.where(ids == row, total, 0.0)

    @pl.when(at == last)
    def _():
        def settle():
            for image in range(sent_s.shape[0]):
                for item in ride(image):
                    item.wait_send()
                for end in range(2):
                    edge = ride_halo.at[end, image]
                    row_copy(
                        edge, edge, ride_send.at[end, image], ride_recv.at[end, image],
                        lax.rem(me + 1, bands),
                    ).wait_recv()
            for spot in range(per_band):
                for away in range(bands):
                    band = lax.rem(me + away, bands)
                    left(given[spot].at[band], out_send.at[spot, away], out_recv.at[0, 0], band)
                    arrived(back_ref.at[spot, band], back_send.at[0, 0], back_recv.at[spot, band], band)
            for image in range(sent_s.shape[0]):
                for head in range(HEADS):
                    left(
                        sent_s.at[image, head], back_send.at[image, head], back_recv.at[0, 0],
                        (head * sent_s.shape[0] + image) // per_band,
                    )

        pieces = feed_pieces(channels, 2 * hidden, hidden, bands)

        def put(place_of, band):
            for total, parts in zip((geglu_s, feed_s, proj_s, attn_s), pieces):
                for at_col, (first, size) in enumerate(parts):
                    if total is feed_s:
                        part = turned_s[pl.ds(pl.multiple_of(band * size, 16), size)]
                    else:
                        part = total[
                            pl.ds(pl.multiple_of(band * size, 16), size),
                            at_col * channels : (at_col + 1) * channels,
                        ]
                    ref, own, skip = place_of(first)
                    ref[own + (pl.ds(first - skip, size),)] = part.astype(BF)

        for first in range(0, hidden, step):
            turned_s[first : first + step, :] = feed_s[:, first : first + step].T.astype(BF)

        if not halving:
            for band in range(bands):
                put(lambda first, band=band: (grads_ref[0], (band,), 0), band)
            settle()
            return
        rows = given_s.shape[-2] // 2
        for apart in range(bands // 2):
            own = (apart & 1, apart >> 1)
            put(lambda first, own=own: (given_s, own, 0), jnp.bitwise_xor(me, 2 * apart + 1))
        item = row_copy(given_s, taken_s, pair_sems.at[0], pair_sems.at[1], jnp.bitwise_xor(me, 1))
        item.start()
        for apart in range(bands // 2):
            over_x, over_y = apart & 1, apart >> 1

            def half(first, over_x=over_x, over_y=over_y):
                return (
                    (grads_ref[over_x], (over_y,), 0)
                    if first < rows
                    else (grads_ref[2 + over_y], (over_x,), rows)
                )

            put(half, jnp.bitwise_xor(me, 2 * apart))
        item.wait()
        for apart in range(bands // 2):
            over_x, over_y = apart & 1, apart >> 1
            for ref, spot, lines in (
                (grads_ref[over_x], over_y, slice(0, rows)),
                (grads_ref[2 + over_y], over_x, slice(rows, 2 * rows)),
            ):
                ref[spot] = (ref[spot].astype(F32) + taken_s[over_x, over_y, lines].astype(F32)).astype(BF)
        settle()


def feed(place, sides, mixed, stream, residual, cot, cross, attn, attn_bias, ln_gain, ln_bias, geglu,
         geglu_bias, feed_out, feed_bias, proj, proj_bias, width, bands, halving):
    images, tokens, channels = stream.shape
    tok = image_block(tokens, channels)
    vector = vector_block(channels)
    table = table_block(channels)
    half = tokens // 2
    per_band = len(mixed)
    anywhere = pl.BlockSpec(memory_space=pl.ANY)
    wide = geglu.shape[1]
    weights = (geglu, feed_out, proj, attn)
    rows = sum(w.size for w in weights) // channels // bands
    lead = (2, 2) if halving else (bands,)
    grads = lead + (rows, channels)
    given = [(2, rows // 2, channels)] * 4 if halving else [grads]
    return pl.pallas_call(
        partial(feed_kernel, width, bands, per_band, halving),
        grid=(images,),
        out_shape=(
            jax.ShapeDtypeStruct(stream.shape, BF),
            jax.ShapeDtypeStruct(stream.shape, F32),
            jax.ShapeDtypeStruct((per_band, bands, half, 128), BF),
            jax.ShapeDtypeStruct((2, images, width, channels), BF),
        )
        + tuple(jax.ShapeDtypeStruct(shape, BF) for shape in given)
        + (
            jax.ShapeDtypeStruct((8, channels), F32),
            jax.ShapeDtypeStruct((8, channels), F32),
            jax.ShapeDtypeStruct((1, wide), F32),
        ),
        in_specs=[
            SMEM_WHOLE,
            SMEM_WHOLE,
        ]
        + [anywhere] * (per_band + 1)
        + [
            tok,
            tok,
            tok,
            table,
            fixed_block(attn.shape),
            vector,
            vector,
            vector,
            anywhere,
            vector_block(wide),
            anywhere,
            vector,
            fixed_block(proj.shape),
            vector,
        ],
        out_specs=(tok, tok, anywhere, anywhere)
        + tuple(fixed_block(shape) for shape in given)
        + (table, table, table_block(wide, 1)),
        scratch_shapes=[
            pltpu.VMEM(geglu.shape, F32),
            pltpu.VMEM(feed_out.shape[::-1], F32),
            pltpu.VMEM(proj.shape, F32),
            pltpu.VMEM(attn.shape, F32),
            pltpu.VMEM(geglu.shape, BF),
            pltpu.VMEM(feed_out.shape, BF),
            pltpu.SemaphoreType.DMA((2,)),
            pltpu.SemaphoreType.DMA((2, images)),
            pltpu.SemaphoreType.DMA((2, images)),
            pltpu.VMEM(feed_out.shape, BF),
        ]
        + [pltpu.VMEM((images, HEADS, half, 128), BF)] * 2
        + [
            pltpu.SemaphoreType.DMA((per_band, bands)),
            pltpu.SemaphoreType.DMA((images, HEADS)),
            pltpu.SemaphoreType.DMA((images, HEADS)),
            pltpu.SemaphoreType.DMA((per_band, bands)),
        ]
        + ([pltpu.VMEM(grads, BF)] * 2 + [pltpu.SemaphoreType.DMA((2,))] if halving else []),
        compiler_params=pltpu.CompilerParams(
            vmem_limit_bytes=62 << 20, collective_id=5, has_side_effects=True
        ),
        name="feed",
    )(place, sides, *mixed, cot, stream, residual, cot, cross, attn, attn_bias, ln_gain, ln_bias, geglu,
      geglu_bias, feed_out, feed_bias, proj, proj_bias)


def leave_kernel(width, bands, images, place, sides, *refs):
    direct = bands == HEADS
    if direct:
        *arrays, raw_ref = refs[:images]
        refs = refs[images:]
    else:
        packed_ref, refs = refs[0], refs[1:]
    (stream_ref, three_ref, field_ref, avg_ref, gain_ref, bias_ref, proj_ref, ln_gain, ln_bias,
     qkv_ref, out_ref, next_avg, next_halo, stats_ref, sums_ref, grad_qkv, grad_proj, qkv_s,
     proj_s, turned_s) = refs[:20]
    scratch = refs[20:26]
    me = lax.axis_index("rows")
    at = pl.program_id(0)
    last = pl.num_programs(0) - 1
    _, tokens, channels = stream_ref.shape
    inside = pixel_inside((tokens, channels), place[0], sides[at], width)

    @pl.when(at == 0)
    def _():
        greet_rows(me, bands)
        for ref in (stats_ref, sums_ref, qkv_s, proj_s):
            ref[...] = jnp.zeros_like(ref)
        turn_qkv(qkv_ref, turned_s)

    if direct:
        item_s, last_s, item_sems, last_send, last_recv = refs[26:]
        fetch = [
            pltpu.make_async_copy(array, item_s.at[image % 2], item_sems.at[image % 2])
            for image, array in enumerate(arrays)
        ]
        send_last = [
            row_copy(
                raw_ref.at[lax.rem(me + away, bands)], last_s.at[me], last_send.at[away], last_recv.at[me],
                lax.rem(me + away, bands),
            )
            for away in range(1, bands)
        ]
        keep_last = pltpu.make_async_copy(raw_ref.at[me], last_s.at[me], last_recv.at[me])

        @pl.when(at == 0)
        def _():
            fetch[0].start()
            meet_rows(bands)
            for item in send_last:
                item.start()
            keep_last.start()

        for image in range(len(fetch)):

            @pl.when(at == image)
            def _(image=image):
                if image + 1 < len(fetch):
                    fetch[image + 1].start()
                fetch[image].wait()

        @pl.when(at == last)
        def _():
            keep_last.wait()
            for away in range(1, bands):
                source = lax.rem(me + away, bands)
                row_copy(
                    last_s.at[source], last_s.at[source], last_send.at[away], last_recv.at[source], source
                ).wait_recv()
            item_s[(images - 1) % 2] = last_s[...]
            for item in send_last:
                item.wait_send()

        packed_ref, spot = item_s, lax.rem(at, 2)
    else:
        spot = 0
    queries = join_heads(packed_ref.at[:, :, tokens:, :], spot)
    joint = jnp.concatenate([packed_ref[spot, head, :tokens] for head in range(HEADS)] + [queries], axis=1)
    centred, inv_std = layer_stats(stream_ref[0])
    attn_in = (centred * vec(ln_gain) + vec(ln_bias)).astype(BF)
    qkv_s[...] += dot_tn(attn_in, joint)
    grads = dot_nt(joint, turned_s[...])
    grad_stream = three_ref[0] + layer_back(grads, vec(ln_gain), centred, inv_std)
    low_in = grad_stream.astype(BF)
    mean, deviation = moments(avg_ref, at)
    normed = (field_ref[0] - mean) * deviation
    flat = (normed * vec(gain_ref) + vec(bias_ref)).astype(BF)
    proj_s[...] += dot_tn(flat, low_in)
    moved = jnp.where(inside, dot_nt(low_in, proj_ref[...]), 0.0)
    out_ref[0] = moved
    share_edges(moved, at, width, next_halo, scratch, me, bands, direct)
    put_row(stats_ref, 2 * at, col_sum(moved))
    put_row(stats_ref, 2 * at + 1, col_sum(moved * normed))
    ids = lax.broadcasted_iota(jnp.int32, sums_ref.shape, 0)
    for row, total in enumerate((col_sum(grads * centred), col_sum(grads), col_sum(grad_stream))):
        sums_ref[...] += jnp.where(ids == row, total, 0.0)

    @pl.when(at == last)
    def _():
        close_exchange(stats_ref[...], gain_ref, sides, next_avg, next_halo, scratch, me, bands)
        grad_qkv[...] = qkv_s[...].astype(BF)
        grad_proj[...] = proj_s[...].astype(BF)


def leave(place, sides, packed, stream, three, field, avg, gain, bias, proj, ln_gain, ln_bias, qkv, width,
          bands):
    images, tokens, channels = stream.shape
    direct = bands == HEADS
    tok = image_block(tokens, channels)
    vector = vector_block(channels)
    table = table_block(channels)
    return pl.pallas_call(
        partial(leave_kernel, width, bands, images),
        grid=(images,),
        out_shape=(
            jax.ShapeDtypeStruct(stream.shape, F32),
            jax.ShapeDtypeStruct((8, channels), F32),
            jax.ShapeDtypeStruct((2, images, width, channels), BF),
            jax.ShapeDtypeStruct((8, channels), F32),
            jax.ShapeDtypeStruct((8, channels), F32),
            jax.ShapeDtypeStruct(qkv.shape, BF),
            jax.ShapeDtypeStruct(proj.shape, BF),
        ),
        in_specs=[
            SMEM_WHOLE,
            SMEM_WHOLE,
        ]
        + (
            [pl.BlockSpec(memory_space=pl.ANY)] * images
            if direct
            else [pl.BlockSpec((1,) + packed[0].shape[1:], lambda at: (at, 0, 0, 0))]
        )
        + [
            tok,
            tok,
            tok,
            table,
            vector,
            vector,
            fixed_block(proj.shape),
            vector,
            vector,
            fixed_block(qkv.shape),
        ],
        out_specs=(
            tok,
            table,
            pl.BlockSpec(memory_space=pl.ANY),
            table,
            table,
            fixed_block(qkv.shape),
            fixed_block(proj.shape),
        ),
        scratch_shapes=[
            pltpu.VMEM(qkv.shape, F32), pltpu.VMEM(proj.shape, F32), pltpu.VMEM(qkv.shape, BF)
        ]
        + exchange_scratch(images, width, channels, bands)
        + (
            [
                pltpu.VMEM((2,) + packed[0].shape, BF),
                pltpu.VMEM(packed[0].shape, BF),
                pltpu.SemaphoreType.DMA((2,)),
                pltpu.SemaphoreType.DMA((bands,)),
                pltpu.SemaphoreType.DMA((bands,)),
            ]
            if direct
            else []
        ),
        compiler_params=pltpu.CompilerParams(
            vmem_limit_bytes=62 << 20, collective_id=7, has_side_effects=True
        ),
        name="leave",
    )(place, sides, *packed, stream, three, field, avg, gain, bias, proj, ln_gain, ln_bias, qkv)

def rounded(field):
    return field.astype(BF)


def join_sums(table_ref, cross, hidden, first, second, third, residual, leaves, feeds, pairs):
    images = cross.shape[0] // 2
    channels = cross.shape[1]
    ids = lax.broadcasted_iota(jnp.int32, cross.shape, 0)

    def total(ref, step, offset, count):
        return col_sum(jnp.where((ids < count) & (lax.rem(ids, step) == offset), ref[...], 0.0))

    rows = [row_of(cross[...], at) for at in range(images)] + [row_of(hidden[...], at) for at in range(images)]
    for ref in (first, second, third):
        rows += [total(ref, 2, 1, 2 * images), total(ref, 2, 0, 2 * images)]
    rows.append(total(residual, 1, 0, images))
    rows += [row_of(leaves[...], at) for at in range(3)] + [row_of(feeds[...], at) for at in range(4)]
    rows += [pairs[:, first : first + channels] for first in range(0, pairs.shape[1], channels)]
    table_ref[...] = jnp.zeros_like(table_ref)
    for at, row in enumerate(rows):
        put_row(table_ref.at[pl.ds(at // 8 * 8, 8)], at % 8, row)


def reduce_kernel(count, bands, groups, *refs):
    last_ref, bands_refs = refs[0], refs[1 : 1 + count]
    half_ref, tables = refs[1 + count], refs[2 + count : 11 + count]
    refs = refs[11 + count :]
    last_out, bands_outs, (gathered, other_ref) = refs[0], refs[1 : 1 + count], refs[1 + count : 3 + count]
    refs = refs[3 + count :]
    table_ref, slots, table_send, table_recv, far_send, far_recv, half_sems = refs[:7]
    sum_s, fields = refs[7], refs[8 : 8 + count]
    refs = refs[8 + count :]
    me, group = lax.axis_index("rows"), lax.axis_index("heads")
    fold = BandFold([last_ref], refs[:9], me)
    tree = GroupTree(fields, bands_outs, refs[9 : 11 + 2 * count], group)
    last_tree = GroupTree([sum_s], [last_out], refs[11 + 2 * count :], group)
    row_peers = [lax.rem(me + away, bands) for away in range(1, bands)]
    far_peers = [lax.rem(group + away, groups) for away in range(1, groups)]
    barrier = pltpu.get_barrier_semaphore()
    for axis, peers in (("rows", row_peers), ("heads", far_peers)):
        for peer in peers:
            pl.semaphore_signal(
                barrier, inc=1, device_id={axis: peer}, device_id_type=pl.DeviceIdType.MESH
            )
    for field, ref in zip(fields, bands_refs):
        field[...] = ref[...]
    join_sums(table_ref, *tables)
    pl.semaphore_wait(barrier, bands + groups - 2)

    def copy(src, dst, send, recv, axis, peer):
        return pltpu.make_async_remote_copy(
            src_ref=src,
            dst_ref=dst,
            send_sem=send,
            recv_sem=recv,
            device_id={axis: peer},
            device_id_type=pl.DeviceIdType.MESH,
        )

    near = [
        copy(table_ref, slots.at[away], table_send.at[away], table_recv.at[away], "rows", peer)
        for away, peer in enumerate(row_peers)
    ]
    for item in near:
        item.start()
    fold.start()
    tree.near()
    half = copy(half_ref, other_ref, half_sems.at[0], half_sems.at[1], "heads", jnp.bitwise_xor(group, 1))
    half.start()
    fold.spread()
    for item in near:
        item.wait_recv()
    total = table_ref[...]
    for away in range(bands - 1):
        total = total + slots[away]
    gathered[group] = total
    far = [
        copy(gathered.at[group], gathered.at[group], far_send.at[away], far_recv.at[away], "heads", peer)
        for away, peer in enumerate(far_peers)
    ]
    for item in far:
        item.start()
    tree.far()
    fold.second()
    fold.finish([sum_s])
    last_tree.near()
    tree.back()
    last_tree.far()
    last_tree.back()
    for away in range(groups - 1):
        source = lax.rem(group - (away + 1) + groups, groups)
        copy(
            gathered.at[source], gathered.at[source], far_send.at[away], far_recv.at[away], "heads", source
        ).wait_recv()
    tree.end()
    last_tree.end()
    half.wait_recv()
    for item in [half] + near + far:
        item.wait_send()


def reduce_parts(last, parts, half, bands, groups, sums):
    shapes = [part.shape for part in parts]
    own = (last.shape[0] // bands, last.shape[1])
    rows = 2 * (sums[0].shape[0] // 2) + 14 + sums[-1].shape[1] // last.shape[1]
    table = (-(-rows // 8) * 8, last.shape[1])
    return pl.pallas_call(
        partial(reduce_kernel, len(parts), bands, groups),
        out_shape=(jax.ShapeDtypeStruct(own, BF),)
        + tuple(jax.ShapeDtypeStruct(shape, BF) for shape in shapes)
        + (
            jax.ShapeDtypeStruct((groups,) + table, F32),
            jax.ShapeDtypeStruct(half.shape, BF),
        ),
        in_specs=[pl.BlockSpec(memory_space=pl.ANY)] + [VMEM_WHOLE] * (len(parts) + 1 + len(sums)),
        out_specs=(VMEM_WHOLE,) * (len(parts) + 3),
        scratch_shapes=[pltpu.VMEM(table, F32), pltpu.VMEM((bands - 1,) + table, F32)]
        + [pltpu.SemaphoreType.DMA((bands - 1,))] * 2
        + [pltpu.SemaphoreType.DMA((groups - 1,))] * 2
        + [pltpu.SemaphoreType.DMA((2,)), pltpu.VMEM(own, BF)]
        + [pltpu.VMEM(shape, BF) for shape in shapes]
        + fold_scratch([last.shape])
        + tree_scratch(shapes)
        + tree_scratch([own]),
        compiler_params=pltpu.CompilerParams(
            vmem_limit_bytes=62 << 20, collective_id=8, has_side_effects=True
        ),
        name="reduce_parts",
    )(last, *parts, half, *sums)


def halve_rows(kept, given, step):
    pairs = [(band, band ^ (1 << step)) for band in range(8)]
    return rounded(kept.astype(F32) + lax.ppermute(given, "rows", pairs).astype(F32))


def sum_groups(part, step, groups):
    odd = lax.rem(lax.axis_index("heads"), 2)
    near = [(at, at ^ 1) for at in range(groups)]
    far = [(at, at ^ 2) for at in range(groups)]
    if step == 0:
        one, two = part
        kept, sent = jnp.where(odd == 0, one, two), jnp.where(odd == 0, two, one)
        return rounded(kept.astype(F32) + lax.ppermute(sent, "heads", near).astype(F32))
    if step == 1:
        return rounded(part.astype(F32) + lax.ppermute(part, "heads", far).astype(F32))
    other = lax.ppermute(part, "heads", near)
    return jnp.where(odd == 0, jnp.concatenate([part, other]), jnp.concatenate([other, part]))


def finals_kernel(pieces, *refs):
    (odd, conv_two, conv_one, qkv, proj_in, kept, other, table, value, context, hot, embed, cross_out,
     cross_value, out_conv_two, out_conv_one, out_qkv, out_proj_in, out_geglu, out_feed, out_proj_out,
     out_attn_out, out_class, out_cross_value, out_cross_out, out_time, rows_s) = refs
    out_conv_two[...] = conv_two[...].astype(F32)
    out_conv_one[...] = conv_one[...].astype(F32)
    out_proj_in[...] = proj_in[...].astype(F32)
    rows, channels = out_proj_in.shape
    low = lane_ids(rows) < 64
    out_qkv[:, :channels] = qkv[:, 2 * channels :].astype(F32)
    for first in range(0, channels, 128):
        one = qkv[:, 2 * first : 2 * first + 128].astype(F32)
        two = qkv[:, 2 * first + 128 : 2 * first + 256].astype(F32)
        out_qkv[:, channels + first : channels + first + 128] = jnp.where(low, one, swap_halves(two))
        out_qkv[:, 2 * channels + first : 2 * channels + first + 128] = jnp.where(
            low, swap_halves(one), two
        )
    flag = jnp.full((1, channels), odd[0], jnp.int32) == 0
    one, two = kept[...].astype(F32), other[...].astype(F32)
    early = jnp.concatenate([jnp.where(flag, one, two), jnp.where(flag, two, one)], axis=0)
    for at, (first, size) in enumerate(pieces[0]):
        out_geglu[:, at * channels : (at + 1) * channels] = early[first : first + size]
    for out, ((first, size),) in zip((out_feed, out_proj_out, out_attn_out), pieces[1:]):
        out[...] = early[first : first + size]
    per_group = value.shape[0] // table.shape[0]

    def joined(first):
        return jnp.concatenate(
            [table[group, first : first + per_group] for group in range(table.shape[0])], axis=0
        )

    def exact(lhs, rhs, dims):
        return lax.dot_general(lhs, rhs, (dims, ((), ())), precision=HIGH, preferred_element_type=F32)

    crossed, shifted = joined(0), joined(per_group)
    own = pl.ds(pl.multiple_of(odd[1] * rows, 16), rows)
    tile = pl.ds(pl.multiple_of(odd[1] * rows // 128 * 128, 128), 128)
    inner = pl.ds(pl.multiple_of(lax.rem(odd[1] * rows, 128), 16), rows)
    rows_s[...] = exact(value[:, tile].astype(F32), crossed, ((0,), (0,)))
    out_cross_out[...] = rows_s[inner]
    grad_value = exact(crossed, cross_out[...].astype(F32), ((1,), (1,)))
    rows_s[...] = exact(context[:, tile], grad_value, ((0,), (0,)))
    out_cross_value[...] = rows_s[inner]
    grad_context = exact(grad_value, cross_value[own].astype(F32), ((1,), (1,)))
    out_class[...] = exact(hot[...].astype(F32), grad_context, ((0,), (0,)))
    times = out_time.shape[0]
    columns = pl.ds(pl.multiple_of(odd[1] * times, 128), times)
    out_time[...] = exact(embed[:, columns].astype(F32), shifted, ((0,), (0,)))


def finals(odd, parts, kept, other, table, value, context, hot, embed, cross_out, cross_value, pieces):
    conv_two, conv_one, qkv, proj_in = parts
    rows, channels = proj_in.shape
    shapes = [part.shape for part in parts] + [
        (rows, len(pieces[0]) * channels),
        (pieces[1][0][1], channels),
        (rows, channels),
        (rows, channels),
        (hot.shape[1], rows),
        (rows, channels),
        (rows, channels),
        (embed.shape[1] * rows // channels, channels),
    ]
    return pl.pallas_call(
        partial(finals_kernel, pieces),
        out_shape=tuple(jax.ShapeDtypeStruct(shape, F32) for shape in shapes),
        in_specs=[SMEM_WHOLE] + [VMEM_WHOLE] * 13,
        out_specs=(VMEM_WHOLE,) * len(shapes),
        scratch_shapes=[pltpu.VMEM((128, channels), F32)],
        compiler_params=pltpu.CompilerParams(vmem_limit_bytes=62 << 20),
        name="finals",
    )(odd, *parts, kept, other, table, value, context, hot, embed, cross_out, cross_value)


def finish_kernel(width, place, sides, kept_ref, grad_ref, field_ref, avg_ref, back_avg, gain_ref, made_ref,
                  out_ref, pass_ref):
    pass_ref[...] = made_ref[...]
    at = pl.program_id(0)
    mean, inv_std = moments(avg_ref, at)
    back = back_avg[...]
    field_slope = inv_std * inv_std * row_of(back, 2 * at + 1)
    offset = inv_std * row_of(back, 2 * at) - mean * field_slope
    moved = grad_ref[0] * (inv_std * vec(gain_ref)) - field_ref[0].astype(F32) * field_slope - offset
    inside = pixel_inside(moved.shape, place[0], sides[at], width)
    out_ref[0] = jnp.where(inside, kept_ref[0] + moved, 0.0)


def finish(place, sides, kept, grads, field, avg, back_avg, gain, made, width):
    images, tokens, channels = kept.shape
    tok = image_block(tokens, channels)
    table = table_block(channels)
    return pl.pallas_call(
        partial(finish_kernel, width),
        grid=(images,),
        out_shape=(jax.ShapeDtypeStruct(kept.shape, F32), jax.ShapeDtypeStruct(made.shape, BF)),
        in_specs=[SMEM_WHOLE, SMEM_WHOLE, tok, tok, tok, table, table, vector_block(channels), tok],
        out_specs=(tok, tok),
        compiler_params=pltpu.CompilerParams(vmem_limit_bytes=62 << 20),
        name="finish",
    )(place, sides, kept, grads, field, avg, back_avg, gain, made)


def time_features(time_steps, dims):
    half_dim = dims // 2
    frequency = jnp.exp(-math.log(10000.0) * jnp.arange(half_dim, dtype=jnp.float32) / half_dim)
    angles = time_steps.astype(jnp.float32)[:, None] * frequency[None, :]
    return jnp.concatenate([jnp.cos(angles), jnp.sin(angles)], axis=-1)


def pad_rows(table):
    return jnp.pad(table, ((0, 8 - table.shape[0]), (0, 0)))


def to_items(sent, bands):
    images, heads = len(sent), sent[0].shape[0]
    per_band = heads * images // bands
    if bands == heads:
        first, *parts = sent
    else:
        items = jnp.stack(sent, axis=1).reshape((bands, per_band) + sent[0].shape[1:])
        parts = [items[:, at] for at in range(per_band)]
    parts = [lax.all_to_all(part, "rows", split_axis=0, concat_axis=0, tiled=True) for part in parts]
    return [first] + parts if bands == heads else parts


def from_items(results, images, bands):
    if bands == HEADS:
        return [
            lax.all_to_all(result, "rows", split_axis=0, concat_axis=0, tiled=True)
            for result in results[:-1]
        ] + results[-1:]
    back = [
        lax.all_to_all(result, "rows", split_axis=0, concat_axis=0, tiled=True)
        for result in results
    ]
    joint = jnp.stack(back, axis=1)
    return [jnp.swapaxes(joint.reshape((HEADS, images) + joint.shape[2:]), 0, 1)]


def per_device(
    images,
    image_sides,
    labels,
    timesteps,
    cotangent,
    first_gain,
    first_bias,
    conv_one,
    time_proj,
    time_bias,
    second_gain,
    second_bias,
    conv_two,
    conv_bias,
    third_gain,
    third_bias,
    proj_in,
    proj_in_bias,
    attn_gain,
    attn_bias,
    qkv_proj,
    attn_out,
    attn_out_bias,
    class_table,
    cross_value,
    cross_out,
    feed_gain,
    feed_bias,
    geglu_proj,
    geglu_bias,
    feed_out,
    feed_out_bias,
    proj_out,
    proj_out_bias,
):
    image_count, band_rows, width, channels = images.shape
    tokens = band_rows * width
    head_dim = channels // HEADS
    score_scale = head_dim ** (-0.5)
    bands = lax.axis_size("rows")
    groups = lax.axis_size("heads")
    halving = bands == 8 and groups == 4 and channels == 512
    me = lax.axis_index("rows")
    first_image = lax.axis_index("heads") * image_count
    sides = lax.dynamic_slice_in_dim(image_sides, first_image, image_count)
    place = jnp.stack([me * band_rows, me]).astype(jnp.int32)

    field = images.reshape(image_count, tokens, channels)
    cot = cotangent.reshape(image_count, tokens, channels)

    hot = rounded(
        (labels[:, None] == jnp.arange(class_table.shape[0], dtype=jnp.int32)[None, :]).astype(F32)
    )
    context = jnp.dot(hot, class_table, preferred_element_type=F32)
    value = rounded(jnp.dot(rounded(context), cross_value, preferred_element_type=F32))
    cross = jnp.dot(value, cross_out, preferred_element_type=F32)
    cross = pad_rows(lax.dynamic_slice_in_dim(cross, first_image, image_count))
    embed = rounded(jax.nn.silu(time_features(timesteps, time_proj.shape[0])))
    shift = jnp.dot(embed, time_proj, preferred_element_type=F32) + time_bias.astype(F32)
    shift = pad_rows(lax.dynamic_slice_in_dim(shift, first_image, image_count))

    avg_one, halo_images = begin(place, sides, field, width, bands)
    hidden, avg_two, halo_hidden = conv_forward(
        place, sides, field, halo_images, avg_one, first_gain, first_bias, conv_one,
        shift, None, width, bands,
    )
    residual, avg_three, halo_residual = conv_forward(
        place, sides, hidden, halo_hidden, avg_two, second_gain, second_bias, conv_two,
        jnp.broadcast_to(conv_bias.astype(F32), (8, channels)), field, width, bands,
    )
    stream, *sent = entry(
        residual, avg_three, third_gain, third_bias, proj_in, proj_in_bias,
        attn_gain, attn_bias, qkv_proj, bands,
    )
    chunks = to_items(sent, bands)
    first_item = me * len(chunks)
    item_sides = [
        lax.dynamic_slice_in_dim(sides, lax.rem(first_item + at, image_count), 1)
        for at in range(len(chunks))
    ]
    attended = [attend(side, chunk, width, score_scale) for side, chunk in zip(item_sides, chunks)]
    mixed = [pairs for pairs, _, _ in attended]
    (
        output, three, grad_chunks, halo_cot, *feed_grads, feed_sums, cross_sum, pair_sums,
    ) = feed(
        place, sides, mixed, stream, residual, cot, cross, attn_out, attn_out_bias,
        feed_gain, feed_bias, geglu_proj, geglu_bias, feed_out,
        feed_out_bias, proj_out, proj_out_bias, width, bands, halving,
    )
    halved = (feed_grads[0:2], feed_grads[2:4]) if halving else None
    results = []
    for spot, (side, chunk, (_, norms, kept)) in enumerate(zip(item_sides, chunks, attended)):
        if halving and spot in (1, 2):
            halved = [
                halve_rows(kept, given, spot if at == 0 else 3 - spot) for at, (kept, given) in enumerate(halved)
            ]
            *halved, norms = lax.optimization_barrier((*halved, norms))
            halved = [(part[0], part[1]) for part in halved] if spot == 1 else halved
        results.append(attend_back(side, chunk, grad_chunks, spot, norms, kept, width, score_scale))
    grad_qkv = from_items(results, image_count, bands)
    if halving:
        early = halved
    else:
        early = feed_grads[0].reshape((bands,) + feed_grads[0].shape[-2:])
        early = lax.psum_scatter(early, "rows", scatter_dimension=0, tiled=True)[0]
        early = lax.psum(early, "heads")
    moved, back_three, halo_moved, third_sums, leave_sums, grad_qkv_proj, grad_proj_in = leave(
        place, sides, grad_qkv, stream, three, residual, avg_three, third_gain,
        third_bias, proj_in, attn_gain, attn_bias, qkv_proj, width, bands,
    )
    if halving:
        *early, back_three = lax.optimization_barrier((*early, back_three))
        early = sum_groups(early, 0, groups)
    *folded, grad_residual, moved, back_two, second_sums, residual_sums, grad_conv_two, halo_moved = conv_backward(
        place, sides, moved, halo_moved, residual, halo_residual, avg_three, back_three,
        third_gain, cot, halo_cot, conv_two, hidden, avg_two, second_gain,
        second_bias, (grad_qkv_proj, grad_proj_in) if halving else (), (), width, bands,
    )
    if halving:
        early, back_two = lax.optimization_barrier((early, back_two))
        early = sum_groups(early, 1, groups)
    *folded, moved, back_one, first_sums, hidden_sums, grad_conv_one = conv_backward(
        place, sides, moved, halo_moved, hidden, halo_hidden, avg_two, back_two, second_gain,
        None, None, conv_one, field, avg_one, first_gain, first_bias,
        (grad_conv_two,) if halving else (), folded, width, bands,
    )
    if halving:
        early, back_one = lax.optimization_barrier((early, back_one))
    grad_images, output = finish(
        place, sides, grad_residual, moved, field, avg_one, back_one, first_gain, output, width
    )
    grad_images = grad_images.reshape(images.shape)

    def own(whole, axis=0):
        size = whole.shape[axis] // bands
        return lax.dynamic_slice_in_dim(whole, me * size, size, axis)

    def reduced(part):
        part = lax.psum_scatter(part, "rows", scatter_dimension=0, tiled=True)
        return lax.psum(part, "heads").astype(F32)

    used = 2 * image_count
    pieces = feed_pieces(channels, geglu_proj.shape[1], feed_out.shape[0], bands)
    if halving:
        grad_images, first_sums = lax.optimization_barrier((grad_images, first_sums))
        rows_two, rows_qkv, rows_in = folded
        rows_one, rows_two, table, other = reduce_parts(
            grad_conv_one, (rows_two,), early, bands, groups,
            (cross_sum, hidden_sums, first_sums, second_sums, third_sums, residual_sums, leave_sums, feed_sums,
             pair_sums),
        )
        late = (rows_two, rows_one, rows_qkv, rows_in)
        odd = jnp.stack([lax.rem(lax.axis_index("heads"), 2), me]).astype(jnp.int32)
        (
            rows_conv_two, rows_conv_one, rows_qkv, rows_proj_in, rows_geglu, rows_feed, rows_proj_out,
            rows_attn_out, grad_class_table, grad_cross_value, grad_cross_out, grad_time_proj,
        ) = finals(
            odd, late, early, other, table, value, context, hot, embed, cross_out, cross_value,
            pieces,
        )
    else:
        table = jnp.concatenate(
            [
                cross_sum[:image_count],
                hidden_sums[:image_count],
                jnp.stack(
                    [
                        jnp.sum(first_sums[1:used:2], axis=0),
                        jnp.sum(first_sums[0:used:2], axis=0),
                        jnp.sum(second_sums[1:used:2], axis=0),
                        jnp.sum(second_sums[0:used:2], axis=0),
                        jnp.sum(third_sums[1:used:2], axis=0),
                        jnp.sum(third_sums[0:used:2], axis=0),
                        jnp.sum(residual_sums[:image_count], axis=0),
                    ]
                ),
                leave_sums[:3],
                feed_sums[:4],
                pair_sums.reshape(-1, channels),
            ]
        )
        table = jnp.pad(table, ((0, -table.shape[0] % 8), (0, 0)))
        table = lax.all_gather(lax.psum(table, "rows"), "heads")
        rows_conv_two, rows_qkv, rows_proj_in, rows_conv_one = (
            reduced(part) for part in (grad_conv_two, grad_qkv_proj, grad_proj_in, grad_conv_one)
        )
        keys_values = rows_qkv[:, : 2 * channels].reshape(-1, HEADS, 2, head_dim)
        rows_qkv = jnp.concatenate(
            [
                rows_qkv[:, 2 * channels :],
                keys_values[:, :, 0].reshape(-1, channels),
                keys_values[:, :, 1].reshape(-1, channels),
            ],
            axis=1,
        )
        early = early.astype(F32)
        rows_geglu = jnp.concatenate([early[first : first + size] for first, size in pieces[0]], axis=1)
        rows_feed, rows_proj_out, rows_attn_out = (
            early[first : first + size] for ((first, size),) in pieces[1:]
        )
    all_cross = table[:, :image_count].reshape(-1, channels)
    all_shift = table[:, image_count : 2 * image_count].reshape(-1, channels)
    if not halving:
        own_value, own_context = own(value.astype(F32), 1), own(context, 1)
        own_embed, own_cross = own(embed.astype(F32), 1), own(cross_value)
        hot = hot.astype(F32)
        grad_cross_out = jnp.dot(own_value.T, all_cross, precision=HIGH)
        grad_value = jnp.dot(all_cross, cross_out.astype(F32).T, precision=HIGH)
        grad_cross_value = jnp.dot(own_context.T, grad_value, precision=HIGH)
        grad_context = jnp.dot(grad_value, own_cross.astype(F32).T, precision=HIGH)
        grad_class_table = jnp.dot(hot.T, grad_context, precision=HIGH)
        grad_time_proj = jnp.dot(own_embed.T, all_shift, precision=HIGH)
    joint = jnp.concatenate(
        [jnp.sum(table[:, 2 * image_count :], axis=0), jnp.sum(all_cross, axis=0)[None],
         jnp.sum(all_shift, axis=0)[None]]
    )
    mine = own(joint, 1)
    singles = [mine[at] for at in range(14)]
    grad_geglu_bias = own(joint[14 : 14 + geglu_bias.shape[0] // channels].reshape(-1))
    return (
        output.reshape(images.shape),
        grad_images,
        singles[0],
        singles[1],
        rows_conv_one,
        grad_time_proj,
        mine[-1],
        singles[2],
        singles[3],
        rows_conv_two,
        singles[6],
        singles[4],
        singles[5],
        rows_proj_in,
        singles[9],
        singles[7],
        singles[8],
        rows_qkv,
        rows_attn_out,
        mine[-2],
        grad_class_table,
        grad_cross_value,
        grad_cross_out,
        singles[12],
        singles[13],
        rows_geglu,
        grad_geglu_bias,
        rows_feed,
        singles[11],
        rows_proj_out,
        singles[10],
    )


def solution(mesh):
    return jax.shard_map(
        per_device,
        mesh=mesh,
        in_specs=(
            P("heads", "rows", None, None),
            P(),
            P(),
            P(),
            P("heads", "rows", None, None),
            P(),
            P(),
            P(),
            P(),
            P(),
            P(),
            P(),
            P(),
            P(),
            P(),
            P(),
            P(),
            P(),
            P(),
            P(),
            P(),
            P(),
            P(),
            P(),
            P(),
            P(),
            P(),
            P(),
            P(),
            P(),
            P(),
            P(),
            P(),
            P(),
        ),
        out_specs=(
            P("heads", "rows", None, None),
            P("heads", "rows", None, None),
            P("rows"),
            P("rows"),
            P("rows", None),
            P("rows", None),
            P("rows"),
            P("rows"),
            P("rows"),
            P("rows", None),
            P("rows"),
            P("rows"),
            P("rows"),
            P("rows", None),
            P("rows"),
            P("rows"),
            P("rows"),
            P("rows", None),
            P("rows", None),
            P("rows"),
            P(None, "rows"),
            P("rows", None),
            P("rows", None),
            P("rows"),
            P("rows"),
            P("rows", None),
            P("rows"),
            P("rows", None),
            P("rows"),
            P("rows", None),
            P("rows"),
        ),
        check_vma=False,
    )
```

profile of v0, /device:TPU:0, one launch (start us, length us, event | category | flops | bytes accessed | tf_op | source)
XLA Modules:
  0.0 685.7 jit_solution(254986153736796268)
XLA Ops:
  5.7 14.8 %begin.1 = (f32[8,512]{1,0:T(8,128)}, bf16[2,4,64,512]{3,2,1,0:T(8,128)(2,1)}) custom-call(s32[2]{0:T(128)} %pad_add_fusion.place.refs_0_.refs_2_.refs_3_, s32[4]{0:T(128)} %dynamic_slice.35.sides.refs_1_.refs_3_.refs_4_, bf16[4,512,512]{2,1,0:T(8,128)(2,1)} %bitcast.60, bf16[4,512,512]{2,1,0:T(8,128)(2,1)} %bitcast.61), custom_call_target="tpu_custom_call" | custom-call | tf_op jit(solution)/shard_map/begin/pallas_call | solution.py:606
  20.6 22.5 %conv_forward.2 = (f32[4,512,512]{2,1,0:T(8,128)}, f32[8,512]{1,0:T(8,128)}, bf16[2,4,64,512]{3,2,1,0:T(8,128)(2,1)}) custom-call(s32[2]{0:T(128)} %pad_add_fusion.place.refs_0_.refs_2_.refs_3_, s32[4]{0:T(128)} %dynamic_slice.35.sides.refs_1_.refs_3_.refs_4_, bf16[4,512,512]{2,1,0:T(8,128)(2,1)} %bitcast.62, ...), custom_call_target="tpu_custom_call" | custom-call | tf_op jit(solution)/shard_map/conv_forward/pallas_call | solution.py:686
  43.7 21.3 %conv_forward.3 = (f32[4,512,512]{2,1,0:T(8,128)}, f32[8,512]{1,0:T(8,128)}, bf16[2,4,64,512]{3,2,1,0:T(8,128)(2,1)}) custom-call(s32[2]{0:T(128)} %pad_add_fusion.place.refs_0_.refs_2_.refs_3_, s32[4]{0:T(128)} %dynamic_slice.35.sides.refs_1_.refs_3_.refs_4_, f32[4,512,512]{2,1,0:T(8,128)} %get-tuple-element.126.refs_2_.refs_14_.refs_7_, ...), custom_call_target="tpu_custom_call" | custom-call | tf_op jit(solution)/shard_map/conv_forward/pallas_call | solution.py:686
  65.0 24.4 %entry.1 = (f32[4,512,512]{2,1,0:T(8,128)}, bf16[8,768,128]{2,1,0:T(8,128)(2,1)}, bf16[8,768,128]{2,1,0:T(8,128)(2,1)}, bf16[8,768,128]{2,1,0:T(8,128)(2,1)}, bf16[8,768,128]{2,1,0:T(8,128)(2,1)}) custom-call(f32[4,512,512]{2,1,0:T(8,128)} %get-tuple-element.129.field_ref.refs_6_, f32[8,512]{1,0:T(8,128)} %get-tuple-element.130.avg_ref.refs_7_.refs_8_, ...), custom_call_target="tpu_custom_call" | custom-call | tf_op jit(solution)/shard_map/entry/pallas_call | solution.py:1197
  89.5 4.6 all-to-all-start
  97.6 24.7 %attend.4 = (bf16[8,256,128]{2,1,0:T(8,128)(2,1)}, f32[4096,128]{1,0:T(8,128)}, bf16[66816,256]{1,0:T(8,128)(2,1)}) custom-call(s32[1]{0:T(128)} %get-tuple-element.270.side_ref, bf16[8,768,128]{2,1,0:T(8,128)(2,1)} %get-tuple-element.131.qkv_ref), custom_call_target="tpu_custom_call" | custom-call | flops 17179869184 | bytes 8388608 | tf_op jit(solution)/shard_map/attend/pallas_call | solution.py:209
  122.3 4.3 all-to-all-start.1
  126.6 12.6 %attend.5 = (bf16[8,256,128]{2,1,0:T(8,128)(2,1)}, f32[4096,128]{1,0:T(8,128)}, bf16[66816,256]{1,0:T(8,128)(2,1)}) custom-call(s32[1]{0:T(128)} %get-tuple-element.269.side_ref, bf16[8,768,128]{2,1,0:T(8,128)(2,1)} %copy-done.9), custom_call_target="tpu_custom_call" | custom-call | flops 17179869184 | bytes 8388608 | tf_op jit(solution)/shard_map/attend/pallas_call | solution.py:209
  139.3 8.4 %all-to-all-done.1.qkv_ref = bf16[8,768,128]{2,1,0:T(8,128)(2,1)} async-done(((bf16[8,768,128]{2,1,0:T(8,128)(2,1)}), bf16[8,768,128]{2,1,0:T(8,128)(2,1)}, u32[]{:S(2)}, u32[]{:S(2)}) %all-to-all-start.1) | async-done | bytes 1572896 | tf_op jit(solution)/shard_map/all_to_all | solution.py:2036
  147.7 3.6 all-to-all-start.2
  151.2 12.4 %attend.6 = (bf16[8,256,128]{2,1,0:T(8,128)(2,1)}, f32[4096,128]{1,0:T(8,128)}, bf16[66816,256]{1,0:T(8,128)(2,1)}) custom-call(s32[1]{0:T(128)} %get-tuple-element.271.side_ref, bf16[8,768,128]{2,1,0:T(8,128)(2,1)} %all-to-all-done.1.qkv_ref), custom_call_target="tpu_custom_call" | custom-call | flops 17179869184 | bytes 8388608 | tf_op jit(solution)/shard_map/attend/pallas_call | solution.py:209
  163.6 8.6 %all-to-all-done.2.qkv_ref = bf16[8,768,128]{2,1,0:T(8,128)(2,1)S(1)} async-done(((bf16[8,768,128]{2,1,0:T(8,128)(2,1)}), bf16[8,768,128]{2,1,0:T(8,128)(2,1)S(1)}, u32[]{:S(2)}, u32[]{:S(2)}) %all-to-all-start.2) | async-done | bytes 1572896 | tf_op jit(solution)/shard_map/all_to_all | solution.py:2036
  173.3 24.9 %attend.7 = (bf16[8,256,128]{2,1,0:T(8,128)(2,1)}, f32[4096,128]{1,0:T(8,128)}, bf16[66816,256]{1,0:T(8,128)(2,1)}) custom-call(s32[1]{0:T(128)} %get-tuple-element.268.side_ref, bf16[8,768,128]{2,1,0:T(8,128)(2,1)} %copy-done.10), custom_call_target="tpu_custom_call" | custom-call | flops 17179869184 | bytes 8388608 | tf_op jit(solution)/shard_map/attend/pallas_call | solution.py:209
  198.3 88.2 %feed.1 = (bf16[4,512,512]{2,1,0:T(8,128)(2,1)}, f32[4,512,512]{2,1,0:T(8,128)}, bf16[4,8,256,128]{3,2,1,0:T(8,128)(2,1)}, bf16[2,4,64,512]{3,2,1,0:T(8,128)(2,1...) custom-call(s32[2]{0:T(128)} %pad_add_fusion.place.refs_0_.refs_2_.r, ...), custom_call_target="tpu_custom_call" | custom-call | tf_op jit(solution)/shard_map/feed/pallas_call | solution.py:1530
  288.6 42.2 %attend_back.4 = bf16[8,768,128]{2,1,0:T(8,128)(2,1)} custom-call(s32[1]{0:T(128)} %get-tuple-element.270.side_ref, bf16[8,768,128]{2,1,0:T(8,128)(2,1)} %get-tuple-element.131.qkv_ref, bf16[4,8,256,128]{3,2,1,0:T(8,128)(2,1)} %get-tuple-element.140.grad_ref, f32[4096,128]{1,0:T(8,128)} %get-tuple-element.141.norm_ref, ...), custom_call_target="tpu_custom_call" | custom-call | flops 34359738368 | bytes 41943040 | tf_op jit(solution)/shard_map/attend_back/pallas_call | solution.py:347
  330.8 3.7 all-to-all-start.3
  336.1 1.8 add_convert_fusion.1
  337.9 2.0 collective-permute-start.3
  342.2 23.8 %attend_back.5 = bf16[8,768,128]{2,1,0:T(8,128)(2,1)} custom-call(s32[1]{0:T(128)} %get-tuple-element.269.side_ref, bf16[8,768,128]{2,1,0:T(8,128)(2,1)} %copy-done.9, bf16[4,8,256,128]{3,2,1,0:T(8,128)(2,1)} %get-tuple-element.140.grad_ref, f32[4096,128]{1,0:T(8,128)} %get-tuple-element.148.norm_ref, bf16[66816,256]{1,0:T(8,128)(2,1)} %get-tuple-element.149.kept_ref), custom_call_target="tpu_custom_call" | custom-call | flops 34359738368 | bytes 41943040 | tf_op jit(solution)/shard_map/attend_back/pallas_call | solution.py:347
  367.3 2.0 fusion.1
  369.3 4.3 all-to-all-start.4
  373.6 24.0 %attend_back.6 = bf16[8,768,128]{2,1,0:T(8,128)(2,1)} custom-call(s32[1]{0:T(128)} %get-tuple-element.271.side_ref, bf16[8,768,128]{2,1,0:T(8,128)(2,1)} %all-to-all-done.1.qkv_ref, bf16[4,8,256,128]{3,2,1,0:T(8,128)(2,1)} %get-tuple-element.140.grad_ref, f32[4096,128]{1,0:T(8,128)} %get-tuple-element.153.norm_ref, ...), custom_call_target="tpu_custom_call" | custom-call | flops 34359738368 | bytes 41943040 | tf_op jit(solution)/shard_map/attend_back/pallas_call | solution.py:347
  397.6 4.1 all-to-all-start.5
  401.7 51.1 %attend_back.7.refs_3_ = bf16[8,768,128]{2,1,0:T(8,128)(2,1)} custom-call(s32[1]{0:T(128)} %get-tuple-element.268.side_ref, bf16[8,768,128]{2,1,0:T(8,128)(2,1)} %copy-done.10, bf16[4,8,256,128]{3,2,1,0:T(8,128)(2,1)} %get-tuple-element.140.grad_ref, f32[4096,128]{1,0:T(8,128)} %get-tuple-element.155.norm_ref, bf16[66816,256]{1,0:T(8,128)(2,1)} %get-tuple-element.156.kept_ref), custom_call_target="tpu_custom_call" | custom-call | flops 34359738368 | bytes 41943040 | tf_op jit(solution)/shard_map/attend_back/pallas_call | solution.py:347
  454.0 35.1 %leave.1 = (f32[4,512,512]{2,1,0:T(8,128)}, f32[8,512]{1,0:T(8,128)}, bf16[2,4,64,512]{3,2,1,0:T(8,128)(2,1)}, f32[8,512]{1,0:T(8,128)}, f32[8,512]{1,0:T(8,128)...) custom-call(s32[2]{0:T(128)} %pad_add_fusion.place.refs_0_.refs_2_.refs_3_, ...), custom_call_target="tpu_custom_call" | custom-call | tf_op jit(solution)/shard_map/leave/pallas_call | solution.py:1702
  489.2 25.5 %collective-permute-start.4 = (bf16[448,512]{1,0:T(8,128)(2,1)S(1)}, bf16[448,512]{1,0:T(8,128)(2,1)S(1)}, u32[]{:S(2)}, u32[]{:S(2)}) collective-permute-start(bf16[448,512]{1,0:T(8,128)(2,1)S(1)} %broadcast_select_fusion), channel_id=1, source_target_pairs={{0,1},{1,0},{2,3},{3,2},{4,5},{5,4},{6,7},{7,6},{8,9},{9,8},{10,11... | collective-permute-start | bytes 1376264 | tf_op jit(solution)/shard_map/ppermute | solution.py:1908
  514.7 42.8 %conv_backward.2 = (bf16[64,1536]{1,0:T(8,128)(2,1)}, bf16[64,512]{1,0:T(8,128)(2,1)}, f32[4,512,512]{2,1,0:T(8,128)}, f32[4,512,512]{2,1,0:T(8,128)}, f32[8,512...) custom-call(bf16[512,1536]{1,0:T(8,128)(2,1)} %get-tuple-element.158, ...), custom_call_target="tpu_custom_call" | custom-call | tf_op jit(solution)/shard_map/conv_backward/pallas_call | solution.py:1059
  559.1 43.1 %conv_backward.3 = (bf16[576,512]{1,0:T(8,128)(2,1)}, bf16[64,1536]{1,0:T(8,128)(2,1)}, bf16[64,512]{1,0:T(8,128)(2,1)}, f32[4,512,512]{2,1,0:T(8,128)}, f32[8,5...) custom-call(bf16[4608,512]{1,0:T(8,128)(2,1)} %get-tuple-element.169.refs_0_, ...), custom_call_target="tpu_custom_call" | custom-call | tf_op jit(solution)/shard_map/conv_backward/pallas_call | solution.py:1059
  603.1 7.4 %finish.1 = (f32[4,512,512]{2,1,0:T(8,128)}, bf16[4,512,512]{2,1,0:T(8,128)(2,1)}) custom-call(s32[2]{0:T(128)} %pad_add_fusion.place.refs_0_.refs_2_.refs_3_, s32[4]{0:T(128)} %dynamic_slice.35.sides.refs_1_.refs_3_.refs_4_, f32[4,512,512]{2,1,0:T(8,128)} %get-tuple-element.168.kept_ref, f32[4,512,512]{2,1,0:T(8,128)} %get-tuple-element.178.grad_ref, ...), custom_call_target="tpu_custom_call" | custom-call | tf_op jit(solution)/shard_map/finish/pallas_call | solution.py:2006
  610.5 62.2 %reduce_parts.1 = (bf16[576,512]{1,0:T(8,128)(2,1)}, bf16[576,512]{1,0:T(8,128)(2,1)}, f32[4,32,512]{2,1,0:T(8,128)}, bf16[448,512]{1,0:T(8,128)(2,1)}) custom-call(bf16[4608,512]{1,0:T(8,128)(2,1)} %get-tuple-element.187.refs_0_, bf16[576,512]{1,0:T(8,128)(2,1)} %get-tuple-element.188.refs_1_, bf16[448,512]{1,0:T(8,128)(2,1)} %add_convert_fusion.2.refs_2_.refs_5_, ...), custom_call_target="tpu_custom_call" | custom-call | tf_op jit(solution)/shard_map/reduce_parts/pallas_call | solution.py:1871
  674.6 7.6 %finals.1 = (f32[576,512]{1,0:T(8,128)}, f32[576,512]{1,0:T(8,128)}, f32[64,1536]{1,0:T(8,128)}, f32[64,512]{1,0:T(8,128)}, f32[64,4096]{1,0:T(8,128)}, /*index=...) custom-call(s32[2]{0:T(128)} %pad_add_fusion.1.refs_0_, ...), custom_call_target="tpu_custom_call" | custom-call | tf_op jit(solution)/shard_map/finals/pallas_call | solution.py:1978
  682.3 1.9 copy.65
  (87 shorter events, 24.3 us)
Async XLA Ops:
  0.7 4.1 copy-start
  4.2 0.6 copy-start.13
  20.5 22.6 %copy-start.19 = (bf16[512]{0:T(512)(128)(2,1)S(1)}, bf16[512]{0:T(512)(128)(2,1)}, u32[]{:S(2)}) copy-start(bf16[512]{0:T(512)(128)(2,1)} %param.47) | copy-start | bytes 3076
  89.4 4.6 copy-start.17
  89.5 6.1 copy-start.7
  89.5 6.3 copy-start.8
  89.5 7.5 %copy-start.16 = (s32[16]{0:T(128)S(1)}, s32[16]{0:T(128)}, u32[]{:S(2)}) copy-start(s32[16]{0:T(128)} %param.35) | copy-start | bytes 196
  89.5 32.8 %all-to-all-start = ((bf16[8,768,128]{2,1,0:T(8,128)(2,1)}), bf16[8,768,128]{2,1,0:T(8,128)(2,1)S(1)}, u32[]{:S(2)}, u32[]{:S(2)}) async-start(bf16[8,768,128]{2,1,0:T(8,128)(2,1)} %get-tuple-element.133), calls=%async_computation | async-start | bytes 3145728 | tf_op jit(solution)/shard_map/all_to_all | solution.py:2036
  95.5 0.6 copy-start.14
  95.7 0.6 copy-start.15
  122.3 4.3 copy-start.9
  122.3 25.3 %all-to-all-start.1 = ((bf16[8,768,128]{2,1,0:T(8,128)(2,1)}), bf16[8,768,128]{2,1,0:T(8,128)(2,1)}, u32[]{:S(2)}, u32[]{:S(2)}) async-start(bf16[8,768,128]{2,1,0:T(8,128)(2,1)} %get-tuple-element.135), calls=%async_computation.1 | async-start | bytes 3145728 | tf_op jit(solution)/shard_map/all_to_all | solution.py:2036
  147.7 24.5 %all-to-all-start.2 = ((bf16[8,768,128]{2,1,0:T(8,128)(2,1)}), bf16[8,768,128]{2,1,0:T(8,128)(2,1)S(1)}, u32[]{:S(2)}, u32[]{:S(2)}) async-start(bf16[8,768,128]{2,1,0:T(8,128)(2,1)} %get-tuple-element.137), calls=%async_computation.2 | async-start | bytes 3145728 | tf_op jit(solution)/shard_map/all_to_all | solution.py:2036
  172.2 1.1 copy-start.10
  286.5 48.0 %collective-permute-start.1 = (bf16[2,448,512]{2,1,0:T(8,128)(2,1)}, bf16[2,448,512]{2,1,0:T(8,128)(2,1)}, u32[]{:S(2)}, u32[]{:S(2)}) collective-permute-start(bf16[2,448,512]{2,1,0:T(8,128)(2,1)} %get-tuple-element.146), channel_id=1, source_target_pairs={{0,16},{4,20},{8,24},{12,28},{16,0},{20,4},{24,8},{28,12},{1,17},{... | collective-permute-start | bytes 2752520 | tf_op jit(solution)/shard_map/ppermute | solution.py:1898
  288.0 48.0 %collective-permute-start = (bf16[2,448,512]{2,1,0:T(8,128)(2,1)}, bf16[2,448,512]{2,1,0:T(8,128)(2,1)}, u32[]{:S(2)}, u32[]{:S(2)}) collective-permute-start(bf16[2,448,512]{2,1,0:T(8,128)(2,1)} %get-tuple-element.144), channel_id=1, source_target_pairs={{0,8},{4,12},{8,0},{12,4},{16,24},{20,28},{24,16},{28,20},{1,9},{5... | collective-permute-start | bytes 2752520 | tf_op jit(solution)/shard_map/ppermute | solution.py:1898
  330.7 3.8 copy-start.12
  330.8 38.6 %all-to-all-start.3 = ((bf16[8,768,128]{2,1,0:T(8,128)(2,1)}), bf16[8,768,128]{2,1,0:T(8,128)(2,1)S(1)}, u32[]{:S(2)}, u32[]{:S(2)}) async-start(bf16[8,768,128]{2,1,0:T(8,128)(2,1)} %attend_back.4), calls=%async_computation.3 | async-start | bytes 3145728 | tf_op jit(solution)/shard_map/all_to_all | solution.py:2043
  334.5 1.6 copy-start.11
  336.0 1.8 copy-start.5
  337.8 2.0 copy-start.6
  337.9 28.1 %collective-permute-start.3 = (bf16[448,512]{1,0:T(8,128)(2,1)S(1)}, bf16[448,512]{1,0:T(8,128)(2,1)}, u32[]{:S(2)}, u32[]{:S(2)}) collective-permute-start(bf16[448,512]{1,0:T(8,128)(2,1)S(1)} %slice_bitcast_fusion), channel_id=1, source_target_pairs={{0,8},{4,12},{8,0},{12,4},{16,24},{20,28},{24,16},{28,20},{1,9},{5... | collective-permute-start | bytes 1376264 | tf_op jit(solution)/shard_map/ppermute | solution.py:1898
  340.7 26.6 %collective-permute-start.2 = (bf16[448,512]{1,0:T(8,128)(2,1)}, bf16[448,512]{1,0:T(8,128)(2,1)}, u32[]{:S(2)}, u32[]{:S(2)}) collective-permute-start(bf16[448,512]{1,0:T(8,128)(2,1)} %slice_bitcast_fusion.1), channel_id=1, source_target_pairs={{0,16},{4,20},{8,24},{12,28},{16,0},{20,4},{24,8},{28,12},{1,17},{... | collective-permute-start | bytes 1376264 | tf_op jit(solution)/shard_map/ppermute | solution.py:1898
  369.3 28.3 %copy-start.2 = (bf16[8,768,128]{2,1,0:T(8,128)(2,1)}, bf16[8,768,128]{2,1,0:T(8,128)(2,1)S(1)}, u32[]{:S(2)}) copy-start(bf16[8,768,128]{2,1,0:T(8,128)(2,1)S(1)} %all-to-all-done.3.refs_0_) | copy-start | bytes 4718596
  369.3 28.3 %all-to-all-start.4 = ((bf16[8,768,128]{2,1,0:T(8,128)(2,1)}), bf16[8,768,128]{2,1,0:T(8,128)(2,1)}, u32[]{:S(2)}, u32[]{:S(2)}) async-start(bf16[8,768,128]{2,1,0:T(8,128)(2,1)} %attend_back.5), calls=%async_computation.4 | async-start | bytes 3145728 | tf_op jit(solution)/shard_map/all_to_all | solution.py:2043
  397.6 55.2 %all-to-all-start.5 = ((bf16[8,768,128]{2,1,0:T(8,128)(2,1)}), bf16[8,768,128]{2,1,0:T(8,128)(2,1)S(1)}, u32[]{:S(2)}, u32[]{:S(2)}) async-start(bf16[8,768,128]{2,1,0:T(8,128)(2,1)} %attend_back.6), calls=%async_computation.5 | async-start | bytes 3145728 | tf_op jit(solution)/shard_map/all_to_all | solution.py:2043
  452.9 1.1 copy-start.3
  489.2 68.4 %collective-permute-start.4 = (bf16[448,512]{1,0:T(8,128)(2,1)S(1)}, bf16[448,512]{1,0:T(8,128)(2,1)S(1)}, u32[]{:S(2)}, u32[]{:S(2)}) collective-permute-start(bf16[448,512]{1,0:T(8,128)(2,1)S(1)} %broadcast_select_fusion), channel_id=1, source_target_pairs={{0,1},{1,0},{2,3},{3,2},{4,5},{5,4},{6,7},{7,6},{8,9},{9,8},{10,11... | collective-permute-start | bytes 1376264 | tf_op jit(solution)/shard_map/ppermute | solution.py:1908
  514.7 42.9 %copy-start.4 = (bf16[448,512]{1,0:T(8,128)(2,1)S(1)}, bf16[448,512]{1,0:T(8,128)(2,1)}, u32[]{:S(2)}) copy-start(bf16[448,512]{1,0:T(8,128)(2,1)} %fusion.1) | copy-start | bytes 1376260
  514.7 43.7 %copy-start.18 = (s32[16]{0:T(128)S(1)}, s32[16]{0:T(128)}, u32[]{:S(2)}) copy-start(s32[16]{0:T(128)} %param.36) | copy-start | bytes 196
  557.7 44.4 %collective-permute-start.5 = (bf16[448,512]{1,0:T(8,128)(2,1)S(1)}, bf16[448,512]{1,0:T(8,128)(2,1)S(1)}, u32[]{:S(2)}, u32[]{:S(2)}) collective-permute-start(bf16[448,512]{1,0:T(8,128)(2,1)S(1)} %add_convert_fusion.3), channel_id=1, source_target_pairs={{0,2},{1,3},{2,0},{3,1},{4,6},{5,7},{6,4},{7,5},{8,10},{9,11},{10,... | collective-permute-start | bytes 1376264 | tf_op jit(solution)/shard_map/ppermute | solution.py:1910
  674.6 10.9 %copy-start.1 = (bf16[1024,512]{1,0:T(8,128)(2,1)S(1)}, bf16[1024,512]{1,0:T(8,128)(2,1)}, u32[]{:S(2)}) copy-start(bf16[1024,512]{1,0:T(8,128)(2,1)} %param.42) | copy-start | bytes 3145732
where the time goes:
time: 683 us; the launch traced here: 686 us
  Pallas kernels  585 us (86%)
  starting transfers between devices  55.7 us (8%)
  waiting for transfers between devices  17 us (2%)
  other arithmetic  13.2 us (2%)
  local copies, waits for them, and re-layouts  11.1 us (2%)
    pallas_call x4, Pallas kernels, attend_back(): pl.pallas_call(partial(attend_back_kernel, width, scale), out_shape=jax.S...  141 us
    pallas_call x1, Pallas kernels, feed(): pl.pallas_call(partial(feed_kernel, width, bands, per_band, halving), gri...  88.2 us
    pallas_call x2, Pallas kernels, conv_backward(): pl.pallas_call(partial(conv_backward_kernel, width, bands, added, len(lat...  85.9 us
    pallas_call x4, Pallas kernels, attend(): pl.pallas_call(partial(attend_kernel, width, scale), out_shape=(jax.Shape...  74.6 us
    pallas_call x1, Pallas kernels, reduce_parts(): pl.pallas_call(partial(reduce_kernel, len(parts), bands, groups), out_sha...  62.2 us
    pallas_call x2, Pallas kernels, conv_forward(): pl.pallas_call(partial(conv_forward_kernel, width, bands, added), grid=(i...  43.8 us
    pallas_call x1, Pallas kernels, leave(): pl.pallas_call(partial(leave_kernel, width, bands, images), grid=(images,...  35.1 us
    ppermute x1, starting transfers between devices, sum_groups(): lax.ppermute(sent, 'heads', near).astype(F32)  25.5 us
  transfers between devices with their start and end apart: 12, of which 2 were waited for; matrix products, arithmetic and copies ran while one was open for 2% of the time, Pallas kernels for 40%

commit v1 on v0

--- a/solution.py
+++ b/solution.py
@@ -1846,9 +1846,9 @@
         item.start()
     tree.far()
     fold.second()
+    tree.back()
     fold.finish([sum_s])
     last_tree.near()
-    tree.back()
     last_tree.far()
     last_tree.back()
     for away in range(groups - 1):

time: 683 us -> 701 us (1.026); the launches traced: 686 us -> 691 us
  Pallas kernels: 585 us -> 624 us
  starting transfers between devices: 55.7 us -> 31.1 us
  waiting for transfers between devices: 17 us -> 8.4 us
    ppermute x1, starting transfers between devices: 25.5 us -> 0.07 us  [sum_groups(): lax.ppermute(sent, 'heads', near).astype(F32)]
    pallas_call x4, Pallas kernels: 141 us -> 160 us  [attend_back(): pl.pallas_call(partial(attend_back_kernel, width, scale), out_shape=jax.S...]
    pallas_call x4, Pallas kernels: 74.6 us -> 86.5 us  [attend(): pl.pallas_call(partial(attend_kernel, width, scale), out_shape=(jax.Shape...]
    all_to_all x3, waiting for transfers between devices: 17 us -> 8.38 us  [to_items(): lax.all_to_all(part, 'rows', split_axis=0, concat_axis=0, tiled=True)]
  transfers between devices with their start and end apart: 12 -> 12, of which waited for: 2 -> 1; matrix products, arithmetic and copies ran while one was open for 2% -> 2% of each run, Pallas kernels for 40% -> 45%
where the time goes in v1:
time: 701 us; the launch traced here: 691 us
  Pallas kernels  624 us (89%)
  starting transfers between devices  31.1 us (4%)
  other arithmetic  13.2 us (2%)
  local copies, waits for them, and re-layouts  11.1 us (2%)
  waiting for transfers between devices  8.4 us (1%)
    pallas_call x4, Pallas kernels, attend_back(): pl.pallas_call(partial(attend_back_kernel, width, scale), out_shape=jax.S...  160 us
    pallas_call x1, Pallas kernels, feed(): pl.pallas_call(partial(feed_kernel, width, bands, per_band, halving), gri...  89.6 us
    pallas_call x2, Pallas kernels, conv_backward(): pl.pallas_call(partial(conv_backward_kernel, width, bands, added, len(lat...  86.6 us
    pallas_call x4, Pallas kernels, attend(): pl.pallas_call(partial(attend_kernel, width, scale), out_shape=(jax.Shape...  86.5 us
    pallas_call x1, Pallas kernels, reduce_parts(): pl.pallas_call(partial(reduce_kernel, len(parts), bands, groups), out_sha...  68.1 us
    pallas_call x2, Pallas kernels, conv_forward(): pl.pallas_call(partial(conv_forward_kernel, width, bands, added), grid=(i...  43.8 us
    pallas_call x1, Pallas kernels, leave(): pl.pallas_call(partial(leave_kernel, width, bands, images), grid=(images,...  35.1 us
    pallas_call x1, Pallas kernels, entry(): pl.pallas_call(partial(entry_kernel, bands, direct), grid=(images,), out_...  24.4 us
  transfers between devices with their start and end apart: 12, of which 1 were waited for; matrix products, arithmetic and copies ran while one was open for 2% of the time, Pallas kernels for 45%

profile of v1, /device:TPU:0, one launch (start us, length us, event | category | flops | bytes accessed | tf_op | source)
XLA Modules:
  0.0 691.2 jit_solution(1607258956332272736)
XLA Ops:
  5.7 14.8 %begin.1 = (f32[8,512]{1,0:T(8,128)}, bf16[2,4,64,512]{3,2,1,0:T(8,128)(2,1)}) custom-call(s32[2]{0:T(128)} %pad_add_fusion.place.refs_0_.refs_2_.refs_3_, s32[4]{0:T(128)} %dynamic_slice.35.sides.refs_1_.refs_3_.refs_4_, bf16[4,512,512]{2,1,0:T(8,128)(2,1)} %bitcast.60, bf16[4,512,512]{2,1,0:T(8,128)(2,1)} %bitcast.61), custom_call_target="tpu_custom_call" | custom-call | tf_op jit(solution)/shard_map/begin/pallas_call | solution.py:606
  20.6 22.5 %conv_forward.2 = (f32[4,512,512]{2,1,0:T(8,128)}, f32[8,512]{1,0:T(8,128)}, bf16[2,4,64,512]{3,2,1,0:T(8,128)(2,1)}) custom-call(s32[2]{0:T(128)} %pad_add_fusion.place.refs_0_.refs_2_.refs_3_, s32[4]{0:T(128)} %dynamic_slice.35.sides.refs_1_.refs_3_.refs_4_, bf16[4,512,512]{2,1,0:T(8,128)(2,1)} %bitcast.62, ...), custom_call_target="tpu_custom_call" | custom-call | tf_op jit(solution)/shard_map/conv_forward/pallas_call | solution.py:686
  43.7 21.3 %conv_forward.3 = (f32[4,512,512]{2,1,0:T(8,128)}, f32[8,512]{1,0:T(8,128)}, bf16[2,4,64,512]{3,2,1,0:T(8,128)(2,1)}) custom-call(s32[2]{0:T(128)} %pad_add_fusion.place.refs_0_.refs_2_.refs_3_, s32[4]{0:T(128)} %dynamic_slice.35.sides.refs_1_.refs_3_.refs_4_, f32[4,512,512]{2,1,0:T(8,128)} %get-tuple-element.126.refs_2_.refs_14_.refs_7_, ...), custom_call_target="tpu_custom_call" | custom-call | tf_op jit(solution)/shard_map/conv_forward/pallas_call | solution.py:686
  65.0 24.4 %entry.1 = (f32[4,512,512]{2,1,0:T(8,128)}, bf16[8,768,128]{2,1,0:T(8,128)(2,1)}, bf16[8,768,128]{2,1,0:T(8,128)(2,1)}, bf16[8,768,128]{2,1,0:T(8,128)(2,1)}, bf16[8,768,128]{2,1,0:T(8,128)(2,1)}) custom-call(f32[4,512,512]{2,1,0:T(8,128)} %get-tuple-element.129.field_ref.refs_6_, f32[8,512]{1,0:T(8,128)} %get-tuple-element.130.avg_ref.refs_7_.refs_8_, ...), custom_call_target="tpu_custom_call" | custom-call | tf_op jit(solution)/shard_map/entry/pallas_call | solution.py:1197
  89.5 4.6 all-to-all-start
  97.6 24.7 %attend.4 = (bf16[8,256,128]{2,1,0:T(8,128)(2,1)}, f32[4096,128]{1,0:T(8,128)}, bf16[66816,256]{1,0:T(8,128)(2,1)}) custom-call(s32[1]{0:T(128)} %get-tuple-element.270.side_ref, bf16[8,768,128]{2,1,0:T(8,128)(2,1)} %get-tuple-element.131.qkv_ref), custom_call_target="tpu_custom_call" | custom-call | flops 17179869184 | bytes 8388608 | tf_op jit(solution)/shard_map/attend/pallas_call | solution.py:209
  122.3 4.3 all-to-all-start.1
  126.6 12.6 %attend.5 = (bf16[8,256,128]{2,1,0:T(8,128)(2,1)}, f32[4096,128]{1,0:T(8,128)}, bf16[66816,256]{1,0:T(8,128)(2,1)}) custom-call(s32[1]{0:T(128)} %get-tuple-element.269.side_ref, bf16[8,768,128]{2,1,0:T(8,128)(2,1)} %copy-done.9), custom_call_target="tpu_custom_call" | custom-call | flops 17179869184 | bytes 8388608 | tf_op jit(solution)/shard_map/attend/pallas_call | solution.py:209
  139.3 8.4 %all-to-all-done.1.qkv_ref = bf16[8,768,128]{2,1,0:T(8,128)(2,1)} async-done(((bf16[8,768,128]{2,1,0:T(8,128)(2,1)}), bf16[8,768,128]{2,1,0:T(8,128)(2,1)}, u32[]{:S(2)}, u32[]{:S(2)}) %all-to-all-start.1) | async-done | bytes 1572896 | tf_op jit(solution)/shard_map/all_to_all | solution.py:2036
  147.7 3.6 all-to-all-start.2
  151.2 24.2 %attend.6 = (bf16[8,256,128]{2,1,0:T(8,128)(2,1)}, f32[4096,128]{1,0:T(8,128)}, bf16[66816,256]{1,0:T(8,128)(2,1)}) custom-call(s32[1]{0:T(128)} %get-tuple-element.271.side_ref, bf16[8,768,128]{2,1,0:T(8,128)(2,1)} %all-to-all-done.1.qkv_ref), custom_call_target="tpu_custom_call" | custom-call | flops 17179869184 | bytes 8388608 | tf_op jit(solution)/shard_map/attend/pallas_call | solution.py:209
  176.6 24.9 %attend.7 = (bf16[8,256,128]{2,1,0:T(8,128)(2,1)}, f32[4096,128]{1,0:T(8,128)}, bf16[66816,256]{1,0:T(8,128)(2,1)}) custom-call(s32[1]{0:T(128)} %get-tuple-element.268.side_ref, bf16[8,768,128]{2,1,0:T(8,128)(2,1)} %copy-done.10), custom_call_target="tpu_custom_call" | custom-call | flops 17179869184 | bytes 8388608 | tf_op jit(solution)/shard_map/attend/pallas_call | solution.py:209
  201.5 89.6 %feed.1 = (bf16[4,512,512]{2,1,0:T(8,128)(2,1)}, f32[4,512,512]{2,1,0:T(8,128)}, bf16[4,8,256,128]{3,2,1,0:T(8,128)(2,1)}, bf16[2,4,64,512]{3,2,1,0:T(8,128)(2,1...) custom-call(s32[2]{0:T(128)} %pad_add_fusion.place.refs_0_.refs_2_.r, ...), custom_call_target="tpu_custom_call" | custom-call | tf_op jit(solution)/shard_map/feed/pallas_call | solution.py:1530
  291.1 1.5 collective-permute-start.1
  294.1 42.2 %attend_back.4 = bf16[8,768,128]{2,1,0:T(8,128)(2,1)} custom-call(s32[1]{0:T(128)} %get-tuple-element.270.side_ref, bf16[8,768,128]{2,1,0:T(8,128)(2,1)} %get-tuple-element.131.qkv_ref, bf16[4,8,256,128]{3,2,1,0:T(8,128)(2,1)} %get-tuple-element.140.grad_ref, f32[4096,128]{1,0:T(8,128)} %get-tuple-element.141.norm_ref, ...), custom_call_target="tpu_custom_call" | custom-call | flops 34359738368 | bytes 41943040 | tf_op jit(solution)/shard_map/attend_back/pallas_call | solution.py:347
  336.2 3.7 all-to-all-start.3
  340.0 1.5 add_convert_fusion
  341.6 1.8 add_convert_fusion.1
  343.4 2.0 collective-permute-start.3
  347.6 23.8 %attend_back.5 = bf16[8,768,128]{2,1,0:T(8,128)(2,1)} custom-call(s32[1]{0:T(128)} %get-tuple-element.269.side_ref, bf16[8,768,128]{2,1,0:T(8,128)(2,1)} %copy-done.9, bf16[4,8,256,128]{3,2,1,0:T(8,128)(2,1)} %get-tuple-element.140.grad_ref, f32[4096,128]{1,0:T(8,128)} %get-tuple-element.148.norm_ref, bf16[66816,256]{1,0:T(8,128)(2,1)} %get-tuple-element.149.kept_ref), custom_call_target="tpu_custom_call" | custom-call | flops 34359738368 | bytes 41943040 | tf_op jit(solution)/shard_map/attend_back/pallas_call | solution.py:347
  372.8 2.0 fusion.1
  374.8 4.3 all-to-all-start.4
  379.1 42.8 %attend_back.6 = bf16[8,768,128]{2,1,0:T(8,128)(2,1)} custom-call(s32[1]{0:T(128)} %get-tuple-element.271.side_ref, bf16[8,768,128]{2,1,0:T(8,128)(2,1)} %all-to-all-done.1.qkv_ref, bf16[4,8,256,128]{3,2,1,0:T(8,128)(2,1)} %get-tuple-element.140.grad_ref, f32[4096,128]{1,0:T(8,128)} %get-tuple-element.153.norm_ref, ...), custom_call_target="tpu_custom_call" | custom-call | flops 34359738368 | bytes 41943040 | tf_op jit(solution)/shard_map/attend_back/pallas_call | solution.py:347
  422.0 4.1 all-to-all-start.5
  426.1 51.1 %attend_back.7.refs_3_ = bf16[8,768,128]{2,1,0:T(8,128)(2,1)} custom-call(s32[1]{0:T(128)} %get-tuple-element.268.side_ref, bf16[8,768,128]{2,1,0:T(8,128)(2,1)} %copy-done.10, bf16[4,8,256,128]{3,2,1,0:T(8,128)(2,1)} %get-tuple-element.140.grad_ref, f32[4096,128]{1,0:T(8,128)} %get-tuple-element.155.norm_ref, bf16[66816,256]{1,0:T(8,128)(2,1)} %get-tuple-element.156.kept_ref), custom_call_target="tpu_custom_call" | custom-call | flops 34359738368 | bytes 41943040 | tf_op jit(solution)/shard_map/attend_back/pallas_call | solution.py:347
  478.4 35.1 %leave.1 = (f32[4,512,512]{2,1,0:T(8,128)}, f32[8,512]{1,0:T(8,128)}, bf16[2,4,64,512]{3,2,1,0:T(8,128)(2,1)}, f32[8,512]{1,0:T(8,128)}, f32[8,512]{1,0:T(8,128)...) custom-call(s32[2]{0:T(128)} %pad_add_fusion.place.refs_0_.refs_2_.refs_3_, ...), custom_call_target="tpu_custom_call" | custom-call | tf_op jit(solution)/shard_map/leave/pallas_call | solution.py:1702
  513.6 42.9 %conv_backward.2 = (bf16[64,1536]{1,0:T(8,128)(2,1)}, bf16[64,512]{1,0:T(8,128)(2,1)}, f32[4,512,512]{2,1,0:T(8,128)}, f32[4,512,512]{2,1,0:T(8,128)}, f32[8,512...) custom-call(bf16[512,1536]{1,0:T(8,128)(2,1)} %get-tuple-element.158, ...), custom_call_target="tpu_custom_call" | custom-call | tf_op jit(solution)/shard_map/conv_backward/pallas_call | solution.py:1059
  558.1 43.8 %conv_backward.3 = (bf16[576,512]{1,0:T(8,128)(2,1)}, bf16[64,1536]{1,0:T(8,128)(2,1)}, bf16[64,512]{1,0:T(8,128)(2,1)}, f32[4,512,512]{2,1,0:T(8,128)}, f32[8,5...) custom-call(bf16[4608,512]{1,0:T(8,128)(2,1)} %get-tuple-element.169.refs_0_, ...), custom_call_target="tpu_custom_call" | custom-call | tf_op jit(solution)/shard_map/conv_backward/pallas_call | solution.py:1059
  602.7 7.4 %finish.1 = (f32[4,512,512]{2,1,0:T(8,128)}, bf16[4,512,512]{2,1,0:T(8,128)(2,1)}) custom-call(s32[2]{0:T(128)} %pad_add_fusion.place.refs_0_.refs_2_.refs_3_, s32[4]{0:T(128)} %dynamic_slice.35.sides.refs_1_.refs_3_.refs_4_, f32[4,512,512]{2,1,0:T(8,128)} %get-tuple-element.168.kept_ref, f32[4,512,512]{2,1,0:T(8,128)} %get-tuple-element.178.grad_ref, ...), custom_call_target="tpu_custom_call" | custom-call | tf_op jit(solution)/shard_map/finish/pallas_call | solution.py:2006
  610.2 68.1 %reduce_parts.1 = (bf16[576,512]{1,0:T(8,128)(2,1)}, bf16[576,512]{1,0:T(8,128)(2,1)}, f32[4,32,512]{2,1,0:T(8,128)}, bf16[448,512]{1,0:T(8,128)(2,1)}) custom-call(bf16[4608,512]{1,0:T(8,128)(2,1)} %get-tuple-element.187.refs_0_, bf16[576,512]{1,0:T(8,128)(2,1)} %get-tuple-element.188.refs_1_, bf16[448,512]{1,0:T(8,128)(2,1)} %add_convert_fusion.2.refs_2_.refs_5_, ...), custom_call_target="tpu_custom_call" | custom-call | tf_op jit(solution)/shard_map/reduce_parts/pallas_call | solution.py:1871
  680.2 7.6 %finals.1 = (f32[576,512]{1,0:T(8,128)}, f32[576,512]{1,0:T(8,128)}, f32[64,1536]{1,0:T(8,128)}, f32[64,512]{1,0:T(8,128)}, f32[64,4096]{1,0:T(8,128)}, /*index=...) custom-call(s32[2]{0:T(128)} %pad_add_fusion.1.refs_0_, ...), custom_call_target="tpu_custom_call" | custom-call | tf_op jit(solution)/shard_map/finals/pallas_call | solution.py:1978
  687.8 1.9 copy.65
  (87 shorter events, 22.2 us)
Async XLA Ops:
  0.7 4.1 copy-start
  4.2 0.6 copy-start.13
  20.5 22.6 %copy-start.19 = (bf16[512]{0:T(512)(128)(2,1)S(1)}, bf16[512]{0:T(512)(128)(2,1)}, u32[]{:S(2)}) copy-start(bf16[512]{0:T(512)(128)(2,1)} %param.47) | copy-start | bytes 3076
  89.4 4.6 copy-start.17
  89.5 6.1 copy-start.7
  89.5 6.3 copy-start.8
  89.5 7.5 %copy-start.16 = (s32[16]{0:T(128)S(1)}, s32[16]{0:T(128)}, u32[]{:S(2)}) copy-start(s32[16]{0:T(128)} %param.35) | copy-start | bytes 196
  89.5 32.8 %all-to-all-start = ((bf16[8,768,128]{2,1,0:T(8,128)(2,1)}), bf16[8,768,128]{2,1,0:T(8,128)(2,1)S(1)}, u32[]{:S(2)}, u32[]{:S(2)}) async-start(bf16[8,768,128]{2,1,0:T(8,128)(2,1)} %get-tuple-element.133), calls=%async_computation | async-start | bytes 3145728 | tf_op jit(solution)/shard_map/all_to_all | solution.py:2036
  95.5 0.6 copy-start.14
  95.7 0.6 copy-start.15
  122.3 4.3 copy-start.9
  122.3 25.3 %all-to-all-start.1 = ((bf16[8,768,128]{2,1,0:T(8,128)(2,1)}), bf16[8,768,128]{2,1,0:T(8,128)(2,1)}, u32[]{:S(2)}, u32[]{:S(2)}) async-start(bf16[8,768,128]{2,1,0:T(8,128)(2,1)} %get-tuple-element.135), calls=%async_computation.1 | async-start | bytes 3145728 | tf_op jit(solution)/shard_map/all_to_all | solution.py:2036
  147.7 27.8 %all-to-all-start.2 = ((bf16[8,768,128]{2,1,0:T(8,128)(2,1)}), bf16[8,768,128]{2,1,0:T(8,128)(2,1)S(1)}, u32[]{:S(2)}, u32[]{:S(2)}) async-start(bf16[8,768,128]{2,1,0:T(8,128)(2,1)} %get-tuple-element.137), calls=%async_computation.2 | async-start | bytes 3145728 | tf_op jit(solution)/shard_map/all_to_all | solution.py:2036
  175.4 1.1 copy-start.10
  291.1 48.9 %collective-permute-start.1 = (bf16[2,448,512]{2,1,0:T(8,128)(2,1)}, bf16[2,448,512]{2,1,0:T(8,128)(2,1)}, u32[]{:S(2)}, u32[]{:S(2)}) collective-permute-start(bf16[2,448,512]{2,1,0:T(8,128)(2,1)} %get-tuple-element.146), channel_id=1, source_target_pairs={{0,16},{4,20},{8,24},{12,28},{16,0},{20,4},{24,8},{28,12},{1,17},{... | collective-permute-start | bytes 2752520 | tf_op jit(solution)/shard_map/ppermute | solution.py:1898
  292.6 48.9 %collective-permute-start = (bf16[2,448,512]{2,1,0:T(8,128)(2,1)}, bf16[2,448,512]{2,1,0:T(8,128)(2,1)}, u32[]{:S(2)}, u32[]{:S(2)}) collective-permute-start(bf16[2,448,512]{2,1,0:T(8,128)(2,1)} %get-tuple-element.144), channel_id=1, source_target_pairs={{0,8},{4,12},{8,0},{12,4},{16,24},{20,28},{24,16},{28,20},{1,9},{5... | collective-permute-start | bytes 2752520 | tf_op jit(solution)/shard_map/ppermute | solution.py:1898
  336.2 3.8 copy-start.12
  336.2 38.6 %all-to-all-start.3 = ((bf16[8,768,128]{2,1,0:T(8,128)(2,1)}), bf16[8,768,128]{2,1,0:T(8,128)(2,1)S(1)}, u32[]{:S(2)}, u32[]{:S(2)}) async-start(bf16[8,768,128]{2,1,0:T(8,128)(2,1)} %attend_back.4), calls=%async_computation.3 | async-start | bytes 3145728 | tf_op jit(solution)/shard_map/all_to_all | solution.py:2043
  340.0 1.6 copy-start.11
  341.5 1.8 copy-start.5
  343.3 2.0 copy-start.6
  343.4 28.1 %collective-permute-start.3 = (bf16[448,512]{1,0:T(8,128)(2,1)S(1)}, bf16[448,512]{1,0:T(8,128)(2,1)}, u32[]{:S(2)}, u32[]{:S(2)}) collective-permute-start(bf16[448,512]{1,0:T(8,128)(2,1)S(1)} %slice_bitcast_fusion), channel_id=1, source_target_pairs={{0,8},{4,12},{8,0},{12,4},{16,24},{20,28},{24,16},{28,20},{1,9},{5... | collective-permute-start | bytes 1376264 | tf_op jit(solution)/shard_map/ppermute | solution.py:1898
  346.2 26.6 %collective-permute-start.2 = (bf16[448,512]{1,0:T(8,128)(2,1)}, bf16[448,512]{1,0:T(8,128)(2,1)}, u32[]{:S(2)}, u32[]{:S(2)}) collective-permute-start(bf16[448,512]{1,0:T(8,128)(2,1)} %slice_bitcast_fusion.1), channel_id=1, source_target_pairs={{0,16},{4,20},{8,24},{12,28},{16,0},{20,4},{24,8},{28,12},{1,17},{... | collective-permute-start | bytes 1376264 | tf_op jit(solution)/shard_map/ppermute | solution.py:1898
  374.8 47.1 %copy-start.2 = (bf16[8,768,128]{2,1,0:T(8,128)(2,1)}, bf16[8,768,128]{2,1,0:T(8,128)(2,1)S(1)}, u32[]{:S(2)}) copy-start(bf16[8,768,128]{2,1,0:T(8,128)(2,1)S(1)} %all-to-all-done.3.refs_0_) | copy-start | bytes 4718596
  374.8 47.1 %all-to-all-start.4 = ((bf16[8,768,128]{2,1,0:T(8,128)(2,1)}), bf16[8,768,128]{2,1,0:T(8,128)(2,1)}, u32[]{:S(2)}, u32[]{:S(2)}) async-start(bf16[8,768,128]{2,1,0:T(8,128)(2,1)} %attend_back.5), calls=%async_computation.4 | async-start | bytes 3145728 | tf_op jit(solution)/shard_map/all_to_all | solution.py:2043
  422.0 55.2 %all-to-all-start.5 = ((bf16[8,768,128]{2,1,0:T(8,128)(2,1)}), bf16[8,768,128]{2,1,0:T(8,128)(2,1)S(1)}, u32[]{:S(2)}, u32[]{:S(2)}) async-start(bf16[8,768,128]{2,1,0:T(8,128)(2,1)} %attend_back.6), calls=%async_computation.5 | async-start | bytes 3145728 | tf_op jit(solution)/shard_map/all_to_all | solution.py:2043
  477.2 1.1 copy-start.3
  513.5 43.0 %collective-permute-start.4 = (bf16[448,512]{1,0:T(8,128)(2,1)S(1)}, bf16[448,512]{1,0:T(8,128)(2,1)S(1)}, u32[]{:S(2)}, u32[]{:S(2)}) collective-permute-start(bf16[448,512]{1,0:T(8,128)(2,1)S(1)} %broadcast_select_fusion), channel_id=1, source_target_pairs={{0,1},{1,0},{2,3},{3,2},{4,5},{5,4},{6,7},{7,6},{8,9},{9,8},{10,11... | collective-permute-start | bytes 1376264 | tf_op jit(solution)/shard_map/ppermute | solution.py:1908
  513.6 42.9 %copy-start.4 = (bf16[448,512]{1,0:T(8,128)(2,1)S(1)}, bf16[448,512]{1,0:T(8,128)(2,1)}, u32[]{:S(2)}) copy-start(bf16[448,512]{1,0:T(8,128)(2,1)} %fusion.1) | copy-start | bytes 1376260
  513.6 43.8 %copy-start.18 = (s32[16]{0:T(128)S(1)}, s32[16]{0:T(128)}, u32[]{:S(2)}) copy-start(s32[16]{0:T(128)} %param.36) | copy-start | bytes 196
  556.7 45.1 %collective-permute-start.5 = (bf16[448,512]{1,0:T(8,128)(2,1)S(1)}, bf16[448,512]{1,0:T(8,128)(2,1)S(1)}, u32[]{:S(2)}, u32[]{:S(2)}) collective-permute-start(bf16[448,512]{1,0:T(8,128)(2,1)S(1)} %add_convert_fusion.3), channel_id=1, source_target_pairs={{0,2},{1,3},{2,0},{3,1},{4,6},{5,7},{6,4},{7,5},{8,10},{9,11},{10,... | collective-permute-start | bytes 1376264 | tf_op jit(solution)/shard_map/ppermute | solution.py:1910
  680.1 10.9 %copy-start.1 = (bf16[1024,512]{1,0:T(8,128)(2,1)S(1)}, bf16[1024,512]{1,0:T(8,128)(2,1)}, u32[]{:S(2)}) copy-start(bf16[1024,512]{1,0:T(8,128)(2,1)} %param.42) | copy-start | bytes 3145732
